TPU v7x, 32 devices: a whole 2x2x4 slice. The times are simulated.
32 devices in a mesh: wide: 8 (over y, x, core), narrow: 4 (over z).
Axes of the slice: x: 2, y: 2, z: 4, core: 2. Of those that a mesh axis runs over, the one named last changes fastest.
Arguments:
- tokens: bfloat16 [16384, 1024], P(('wide', 'narrow')), may hold values from -6 to 6
- segment_ids: int32 [32, 512], P(('wide', 'narrow')), may hold values from 0 to 7, never falling along the last dimension, each value on 1 to 256 neighbouring positions
- attn_weight: bfloat16 [4096, 1024], P(('wide', 'narrow')), may hold values from -2 to 2, as said below
- vectors: bfloat16 [8192], P(('wide', 'narrow')), may hold values from -3 to 3
- ffn_weight: bfloat16 [2, 1024, 4096], P(None, 'wide', 'narrow'), may hold values from -0.1875 to 0.1875
- ffn_bias: bfloat16 [4096], P(('narrow', 'wide')), may hold values from -3 to 3
- out_grad: bfloat16 [16384, 1024], P(('wide', 'narrow')), may hold values from -6 to 6
Outputs:
- result: bfloat16 [16384, 1024], P(('wide', 'narrow'))
- grad_tokens: float32 [16384, 1024], P(('wide', 'narrow'))
- grad_attn: float32 [4096, 1024], P(('wide', 'narrow'))
- grad_vectors: float32 [8192], P(('wide', 'narrow'))
- grad_ffn: float32 [2, 1024, 4096], P(None, 'wide', 'narrow')
- grad_ffn_bias: float32 [4096], P(('narrow', 'wide'))
Inputs may be any that keep to these rules, and one draw needn't show every extreme that they name: `segment_ids`: within each packed row of 512 tokens the ids never fall; each protein holds 1 to 256 tokens. `attn_weight`: entries drawn independently.
All inputs are finite; a program needn't handle non-finite values.
Results may differ from a plain program's by a relative error of at most 0.017.
Values may be sent and summed in bfloat16 or wider, within the bound.
No kernel may reach another device: no remote copies, remote signals or barrier semaphores. Data moves between devices by JAX's collectives and lax.ppermute only.
A program may use at most 192 MiB of HBM per device.

v0:
```python
import jax
import jax.numpy as jnp
from jax import lax
from jax.sharding import PartitionSpec as P

HEADS = 16
HEAD = 64


contract_last = (((1,), (1,)), ((), ()))
contract_first = (((0,), (0,)), ((), ()))


def split_heads(matrix, batches):
    tokens_count, features = matrix.shape
    length = tokens_count // batches
    return (
        matrix.reshape(batches, length, HEADS, HEAD)
        .transpose(0, 2, 1, 3)
        .reshape(batches * HEADS, length, HEAD)
    )


def merge_heads(stacked, batches):
    length = stacked.shape[1]
    return (
        stacked.reshape(batches, HEADS, length, HEAD)
        .transpose(0, 2, 1, 3)
        .reshape(batches * length, HEADS * HEAD)
    )


def masked_scores(query_head, key_head, segment_row):
    scores = lax.dot_general(
        query_head, key_head, contract_last, preferred_element_type=jnp.float32
    ) * HEAD ** (-0.5)
    allowed = segment_row[:, None] == segment_row[None, :]
    return jnp.where(allowed, scores, -1e30)


def head_forward(members):
    query_head, key_head, value_head, segment_row = members
    scores = masked_scores(query_head, key_head, segment_row)
    highest_score = jnp.max(scores, -1, keepdims=True)
    raised = jnp.exp(scores - highest_score)
    totals = jnp.sum(raised, -1, keepdims=True)
    weights = (raised / totals).astype(jnp.bfloat16)
    mixed_heads = jnp.dot(weights, value_head, preferred_element_type=jnp.float32)
    return (mixed_heads, (highest_score + jnp.log(totals))[:, 0])


def head_backward(members):
    query_head, key_head, value_head, segment_row, grad_head, log_total = members
    weights = jnp.exp(masked_scores(query_head, key_head, segment_row) - log_total[:, None])
    grad_weights = lax.dot_general(
        grad_head, value_head, contract_last, preferred_element_type=jnp.float32
    )
    grad_value = lax.dot_general(
        weights.astype(jnp.bfloat16), grad_head, contract_first, preferred_element_type=jnp.float32
    )
    inner_sum = jnp.sum(weights * grad_weights, -1, keepdims=True)
    grad_scores = (weights * (grad_weights - inner_sum)).astype(jnp.bfloat16)
    grad_query = jnp.dot(grad_scores, key_head, preferred_element_type=jnp.float32) * HEAD ** (-0.5)
    grad_key = lax.dot_general(
        grad_scores, query_head, contract_first, preferred_element_type=jnp.float32
    ) * HEAD ** (-0.5)
    return (grad_query, grad_key, grad_value)


def normalize(hidden):
    center = hidden - jnp.mean(hidden, -1, keepdims=True)
    factor = lax.rsqrt(jnp.mean(center * center, -1, keepdims=True) + 1e-12)
    return (center * factor, factor)


def norm_backward(grad_normed, normed, factor):
    return factor * (
        grad_normed
        - jnp.mean(grad_normed, -1, keepdims=True)
        - normed * jnp.mean(grad_normed * normed, -1, keepdims=True)
    )


def gelu_exact(argument):
    return jax.nn.gelu(argument, approximate=False)


def feed_forward(first_low, ffn_part, bias_part):
    ffn_full, bias_full = (ffn_part, bias_part)
    ffn_rows = lax.all_gather(first_low, "narrow", axis=0, tiled=True)
    w_up = ffn_full[0]
    w_down = ffn_full[1]
    before_act = jnp.dot(ffn_rows, w_up, preferred_element_type=jnp.float32) + bias_full.astype(
        jnp.float32
    )
    active_low = gelu_exact(before_act).astype(jnp.bfloat16)
    ffn_out = lax.psum_scatter(
        lax.dot_general(
            active_low, w_down, contract_last, preferred_element_type=jnp.float32
        ).astype(jnp.bfloat16),
        "narrow",
        scatter_dimension=0,
        tiled=True,
    ).astype(jnp.float32)
    return (ffn_rows, w_up, w_down, before_act, active_low, ffn_out)


def run_forward(tokens, segment_ids, attn_weight, vectors, ffn_weight, ffn_bias):
    attn_full, vector_full = (
        lax.all_gather(attn_weight, ("wide", "narrow"), axis=0, tiled=True),
        lax.all_gather(vectors, ("wide", "narrow"), axis=0, tiled=True),
    )
    ffn_part, bias_part = (
        lax.all_gather(ffn_weight, "wide", axis=1, tiled=True),
        lax.all_gather(ffn_bias, "wide", axis=0, tiled=True),
    )
    features = attn_full.shape[1]
    batches = segment_ids.shape[0]
    vector_rows = vector_full.astype(jnp.float32).reshape(8, features)
    stacked = attn_full[: 3 * features].reshape(3, features, features)
    w_out = attn_full[3 * features :]
    projected = jnp.einsum("td,kde->kte", tokens, stacked, preferred_element_type=jnp.float32)
    query_low = (projected[0] + vector_rows[0]).astype(jnp.bfloat16)
    key_low = projected[1].astype(jnp.bfloat16)
    value_low = (projected[2] + vector_rows[1]).astype(jnp.bfloat16)
    segment_heads = jnp.repeat(segment_ids, HEADS, axis=0)
    query_heads = split_heads(query_low, batches)
    key_heads = split_heads(key_low, batches)
    value_heads = split_heads(value_low, batches)
    head_outs, log_totals = lax.map(
        head_forward, (query_heads, key_heads, value_heads, segment_heads)
    )
    mixed_low = merge_heads(head_outs, batches).astype(jnp.bfloat16)
    first_sum = (
        tokens.astype(jnp.float32)
        + jnp.dot(mixed_low, w_out, preferred_element_type=jnp.float32)
        + vector_rows[2]
    )
    normed_one, factor_one = normalize(first_sum)
    first_norm = normed_one * (1.0 + vector_rows[6]) + vector_rows[3]
    ffn_rows, w_up, w_down, before_act, active_low, ffn_out = feed_forward(
        first_norm.astype(jnp.bfloat16), ffn_part, bias_part
    )
    second_sum = first_norm + ffn_out + vector_rows[4]
    normed_two, factor_two = normalize(second_sum)
    result = (normed_two * (1.0 + vector_rows[7]) + vector_rows[5]).astype(jnp.bfloat16)
    return dict(
        vector_rows=vector_rows,
        stacked=stacked,
        w_out=w_out,
        query_heads=query_heads,
        key_heads=key_heads,
        value_heads=value_heads,
        segment_heads=segment_heads,
        log_totals=log_totals,
        mixed_low=mixed_low,
        normed_one=normed_one,
        factor_one=factor_one,
        ffn_rows=ffn_rows,
        w_up=w_up,
        w_down=w_down,
        before_act=before_act,
        active_low=active_low,
        normed_two=normed_two,
        factor_two=factor_two,
        result=result,
    )


def per_device(tokens, segment_ids, attn_weight, vectors, ffn_weight, ffn_bias, out_grad):
    kept_state = run_forward(tokens, segment_ids, attn_weight, vectors, ffn_weight, ffn_bias)
    inputs = lax.optimization_barrier(
        (tokens, segment_ids, attn_weight, vectors, ffn_weight, ffn_bias, kept_state["result"])
    )
    forward_state = run_forward(inputs[0], inputs[1], inputs[2], inputs[3], inputs[4], inputs[5])
    vector_rows = forward_state["vector_rows"]
    normed_two = forward_state["normed_two"]
    normed_one = forward_state["normed_one"]
    w_up = forward_state["w_up"]
    w_down = forward_state["w_down"]
    grad_out = out_grad.astype(jnp.float32)
    grad_shift_two = jnp.sum(grad_out, 0)
    grad_gain_two = jnp.sum(grad_out * normed_two, 0)
    grad_second = norm_backward(
        grad_out * (1.0 + vector_rows[7]), normed_two, forward_state["factor_two"]
    )
    grad_ffn_shift = jnp.sum(grad_second, 0)
    grad_second_low = grad_second.astype(jnp.bfloat16)
    grad_rows = lax.all_gather(grad_second_low, "narrow", axis=0, tiled=True)
    grad_active = jnp.dot(grad_rows, w_down, preferred_element_type=jnp.float32)
    grad_down = lax.dot_general(
        grad_rows, forward_state["active_low"], contract_first, preferred_element_type=jnp.float32
    )
    unused_value, gelu_pull = jax.vjp(gelu_exact, forward_state["before_act"])
    grad_before = gelu_pull(grad_active)[0]
    bias_terms = jnp.sum(grad_before, 0)
    grad_before_low = grad_before.astype(jnp.bfloat16)
    grad_up = lax.dot_general(
        forward_state["ffn_rows"],
        grad_before_low,
        contract_first,
        preferred_element_type=jnp.float32,
    )
    stack_terms = jnp.stack([grad_up, grad_down])
    row_block = lax.slice_in_dim(
        grad_before_low, 0, tokens.shape[0] * lax.axis_size("narrow"), axis=0
    )
    grad_first_ffn = lax.psum_scatter(
        lax.dot_general(row_block, w_up, contract_last, preferred_element_type=jnp.float32).astype(
            jnp.bfloat16
        ),
        "narrow",
        scatter_dimension=0,
        tiled=True,
    ).astype(jnp.float32)
    grad_ffn, grad_ffn_bias = (
        lax.psum_scatter(
            stack_terms.astype(jnp.bfloat16), "wide", scatter_dimension=1, tiled=True
        ).astype(jnp.float32),
        lax.psum_scatter(
            bias_terms.astype(jnp.bfloat16), "wide", scatter_dimension=0, tiled=True
        ).astype(jnp.float32),
    )
    grad_first = grad_first_ffn + grad_second
    grad_shift_one = jnp.sum(grad_first, 0)
    grad_gain_one = jnp.sum(grad_first * normed_one, 0)
    grad_first_sum = norm_backward(
        grad_first * (1.0 + vector_rows[6]), normed_one, forward_state["factor_one"]
    )
    grad_out_bias = jnp.sum(grad_first_sum, 0)
    grad_sum_low = grad_first_sum.astype(jnp.bfloat16)
    grad_w_out = lax.dot_general(
        forward_state["mixed_low"], grad_sum_low, contract_first, preferred_element_type=jnp.float32
    )
    grad_mixed_low = lax.dot_general(
        grad_sum_low, forward_state["w_out"], contract_last, preferred_element_type=jnp.float32
    ).astype(jnp.bfloat16)
    batches = segment_ids.shape[0]
    grad_q_heads, grad_k_heads, grad_v_heads = lax.map(
        head_backward,
        (
            forward_state["query_heads"],
            forward_state["key_heads"],
            forward_state["value_heads"],
            forward_state["segment_heads"],
            split_heads(grad_mixed_low, batches),
            forward_state["log_totals"],
        ),
    )
    grad_query = merge_heads(grad_q_heads, batches)
    grad_key = merge_heads(grad_k_heads, batches)
    grad_value = merge_heads(grad_v_heads, batches)
    grad_query_bias = jnp.sum(grad_query, 0)
    grad_value_bias = jnp.sum(grad_value, 0)
    grad_proj_low = jnp.stack([grad_query, grad_key, grad_value]).astype(jnp.bfloat16)
    grad_stacked = jnp.einsum(
        "td,kte->kde", tokens, grad_proj_low, preferred_element_type=jnp.float32
    )
    grad_tokens = grad_first_sum + jnp.einsum(
        "kte,kde->td", grad_proj_low, forward_state["stacked"], preferred_element_type=jnp.float32
    )
    features = tokens.shape[1]
    grad_attn_full = jnp.concatenate([grad_stacked.reshape(3 * features, features), grad_w_out], 0)
    grad_vector_full = jnp.stack(
        [
            grad_query_bias,
            grad_value_bias,
            grad_out_bias,
            grad_shift_one,
            grad_ffn_shift,
            grad_shift_two,
            grad_gain_one,
            grad_gain_two,
        ]
    ).reshape(8 * features)
    grad_attn, grad_vectors = (
        lax.psum_scatter(grad_attn_full, ("wide", "narrow"), scatter_dimension=0, tiled=True),
        lax.psum_scatter(grad_vector_full, ("wide", "narrow"), scatter_dimension=0, tiled=True),
    )
    return (kept_state["result"], grad_tokens, grad_attn, grad_vectors, grad_ffn, grad_ffn_bias)


def solution(mesh):
    return jax.shard_map(
        per_device,
        mesh=mesh,
        in_specs=(
            P(("wide", "narrow"), None),
            P(("wide", "narrow"), None),
            P(("wide", "narrow"), None),
            P(("wide", "narrow")),
            P(None, "wide", "narrow"),
            P(("narrow", "wide")),
            P(("wide", "narrow"), None),
        ),
        out_specs=(
            P(("wide", "narrow"), None),
            P(("wide", "narrow"), None),
            P(("wide", "narrow"), None),
            P(("wide", "narrow")),
            P(None, "wide", "narrow"),
            P(("narrow", "wide")),
        ),
        check_vma=False,
    )
```

profile of v0, /device:TPU:0, one launch (start us, length us, event | category | flops | bytes accessed | tf_op | source)
XLA Modules:
  0.0 1397.7 jit_solution(4676478962462997327)
XLA Ops:
  9.5 70.3 %all-gather = bf16[32,1,256]{2,1,0:T(2,128)(2,1)S(1)} all-gather(bf16[1,1,256]{2,1,0:T(2,128)(2,1)S(1)} %reshape.369), channel_id=1, replica_groups=mesh['wide'=8,'narrow'=4] {'wide','narrow'}, dimensions={0}, use_global_device_ids=true | all-gather | bytes 16896 | tf_op jit(solution)/shard_map/all_gather | solution.py:111
  80.1 11.0 all-gather.12.cloned.1.call-done
  113.6 43.0 %while.39 = (s32[]{:T(128)}, bf16[16,512,64]{1,2,0:T(8,128)(2,1)S(1)}, s32[16,512]{1,0:T(8,128)S(1)}, bf16[16,512,64]{2,1,0:T(8,128)(2,1)}, bf16[16,512,64]{2,1,0:T(8,128)(2,1)S(1)}, /*index=5*/bf16[16,512,64]{2,1,0:T(8,128)(2,1)}) while((s32[]{:T(128)}, bf16[16,512,64]{1,2,0:T(8,128)(2,1)S(1)}, s32[16,512]{1,0:T(8,128)S(1)}, ...), condition=%wide.region_3.4_spmd.clone, body=%wide.region_0.3_spmd.sunk.clone | while | flops 69467136 | bytes 3690577 | solution.py:130
  161.7 8.6 all-gather.1
  170.3 70.7 %all-gather.14.cloned.1.call-done = bf16[2048,1024]{1,0:T(8,128)(2,1)} async-done(((bf16[512,1024]{1,0:T(8,128)(2,1)}), bf16[2048,1024]{1,0:T(8,128)(2,1)}) %all-gather.14.cloned.1.call-update) | async-done | bytes 4194320 | tf_op jit(solution)/shard_map/all_gather | solution.py:90
  241.0 29.3 %fusion.73 = bf16[2048,1024]{1,0:T(8,128)(2,1)} fusion(f32[1024]{0:T(1024)S(1)} %bitcast.352, bf16[2048,1024]{1,0:T(8,128)(2,1)} %all-gather.14.cloned.1.call-done, bf16[2,1024,1024]{2,1,0:T(8,128)(2,1)} %all-gather.16.cloned.1.call-done), kind=kOutput, calls=%fused_computation.117 | convolution fusion | flops 8730443776 | bytes 12587008 | tf_op jit(solution)/shard_map/dot_general | solution.py:98
  270.6 75.2 %reduce-scatter.6.cloned.1.call-done = bf16[512,1024]{1,0:T(8,128)(2,1)} async-done(((bf16[2048,1024]{1,0:T(8,128)(2,1)}), bf16[512,1024]{1,0:T(8,128)(2,1)}) %reduce-scatter.6.cloned.1.call-update) | async-done | bytes 1048592 | tf_op jit(solution)/shard_map/reduce_scatter | solution.py:97
  349.7 68.0 %all-gather.2 = bf16[32,1,256]{2,1,0:T(2,128)(2,1)S(1)} all-gather(bf16[1,1,256]{2,1,0:T(2,128)(2,1)S(1)} %reshape.373), channel_id=1, replica_groups=mesh['wide'=8,'narrow'=4] {'wide','narrow'}, dimensions={0}, use_global_device_ids=true | all-gather | bytes 16896 | tf_op jit(solution)/shard_map/all_gather | solution.py:111
  418.0 9.7 all-gather.18.cloned.1.call-done
  450.2 44.2 %while.40 = (s32[]{:T(128)}, bf16[16,512,64]{1,2,0:T(8,128)(2,1)S(1)}, f32[16,512]{1,0:T(8,128)S(1)}, s32[16,512]{1,0:T(8,128)S(1)}, bf16[16,512,64]{2,1,0:T(8,1...) while((s32[]{:T(128)}, bf16[16,512,64]{1,2,0:T(8,128)(2,1)S(1)}, ...), condition=%wide.region_12.13_spmd.clone, body=%wide.region_9.12_spmd.sunk.clone | while | flops 69467648 | bytes 3700829 | solution.py:130
  500.8 9.2 all-gather.3
  510.0 70.4 %all-gather.20.cloned.1.call-done = bf16[2048,1024]{1,0:T(8,128)(2,1)} async-done(((bf16[512,1024]{1,0:T(8,128)(2,1)}), bf16[2048,1024]{1,0:T(8,128)(2,1)}) %all-gather.20.cloned.1.call-update) | async-done | bytes 4194320 | tf_op jit(solution)/shard_map/all_gather | solution.py:90
  580.5 25.9 %multiply_convert_fusion.1 = (bf16[2048,1024]{1,0:T(8,128)(2,1)S(1)}, f32[2048,1024]{1,0:T(8,128)}, f32[2048,1024]{1,0:T(8,128)}) fusion(f32[1024]{0:T(1024)S(1)} %bitcast.350, bf16[2048,1024]{1,0:T(8,128)(2,1)} %all-gather.20.cloned.1.call-done, bf16[2,1024,1024]{2,1,0:T(8,128)(2,1)} %all-gather.22.cloned.1.call-done), kind=kOutput, calls=%fused_computation.82 | convolution fusion | flops 4433379328 | bytes 27267072 | tf_op jit(solution)/shard_map/dot_general | solution.py:93
  614.8 75.4 %reduce-scatter.8.cloned.1.call-done = bf16[512,1024]{1,0:T(8,128)(2,1)} async-done(((bf16[2048,1024]{1,0:T(8,128)(2,1)}), bf16[512,1024]{1,0:T(8,128)(2,1)}) %reduce-scatter.8.cloned.1.call-update) | async-done | bytes 1048592 | tf_op jit(solution)/shard_map/reduce_scatter | solution.py:97
  696.2 81.2 %all-gather.24.cloned.1.call-done = bf16[2048,1024]{1,0:T(8,128)(2,1)} async-done(((bf16[512,1024]{1,0:T(8,128)(2,1)}), bf16[2048,1024]{1,0:T(8,128)(2,1)}) %all-gather.24.cloned.1.call-update) | async-done | bytes 4194320 | tf_op jit(solution)/shard_map/all_gather | solution.py:189
  777.3 14.4 %fusion.166 = (bf16[1024]{0:T(1024)(128)(2,1)S(1)}, bf16[2048,1024]{1,0:T(8,128)(2,1)S(1)}) fusion(f32[2048,1024]{1,0:T(8,128)} %get-tuple-element.234, bf16[2048,1024]{1,0:T(8,128)(2,1)} %all-gather.24.cloned.1.call-done, bf16[2,1024,1024]{2,1,0:T(8,128)(2,1)} %all-gather.22.cloned.1.call-done, f32[2048,1024]{1,0:T(8,128)} %get-tuple-element.265, ...), kind=kOutput, calls=%fused_computation.258 | convolution fusion | flops 4328520704 | bytes 27269120 | tf_op jit(solution)/shard_map/dot_general | solution.py:190
  800.1 8.2 convert_bitcast_fusion
  815.7 59.8 %reduce-scatter.10.cloned.1.call-done = bf16[512,1024]{1,0:T(8,128)(2,1)} async-done(((bf16[2048,1024]{1,0:T(8,128)(2,1)}), bf16[512,1024]{1,0:T(8,128)(2,1)}) %reduce-scatter.10.cloned.1.call-update) | async-done | bytes 1048592 | tf_op jit(solution)/shard_map/reduce_scatter | solution.py:208
  887.2 113.0 %while.41 = (s32[]{:T(128)}, f32[16,512,64]{1,2,0:T(8,128)S(1)}, bf16[16,512,64]{1,2,0:T(8,128)(2,1)S(1)}, f32[16,512,64]{1,2,0:T(8,128)}, s32[16,512]{1,0:T(8,1...) while((s32[]{:T(128)}, f32[16,512,64]{1,2,0:T(8,128)S(1)}, ...), condition=%wide.region_25.26_spmd.clone, body=%wide.region_23.25_spmd.sunk.clone | while | flops 170458624 | bytes 9067637 | solution.py:239
  1017.4 7.2 pad_maximum_fusion
  1026.5 13.9 all-reduce.1
  1046.9 43.8 %all-reduce = f32[8192]{0:T(1024)S(1)} all-reduce(f32[8192]{0:T(1024)S(1)} %bitcast.323), channel_id=6, replica_groups=mesh['wide'=8,'narrow'=4] {'wide','narrow'}, use_global_device_ids=true, to_apply=%region_35.36.clone | all-reduce | flops 8192 | bytes 65536
  1091.4 8.2 bitcast_add_fusion
  1099.6 290.8 %reduce-scatter.12.cloned.1.call-done = f32[128,1024]{1,0:T(8,128)} async-done(((f32[4096,1024]{1,0:T(8,128)}), f32[128,1024]{1,0:T(8,128)}) %reduce-scatter.12.cloned.1.call-update) | async-done | bytes 524304 | tf_op jit(solution)/shard_map/reduce_scatter | solution.py:277
  (467 shorter events, 328.7 us)
Async XLA Ops:
  7.2 84.0 %all-gather.12.cloned.1.call-start = ((), (), s32[]{:S(2)}) async-start(), calls=%async_computation.5 | async-start | bytes 8650752 | tf_op jit(solution)/shard_map/all_gather | solution.py:110
  7.9 162.4 %all-gather.16.cloned.1.call-start = ((), (), s32[]{:S(2)}) async-start(), calls=%async_computation.7 | async-start | bytes 4718592 | tf_op jit(solution)/shard_map/all_gather | solution.py:114
  8.6 232.4 %all-gather.14.cloned.1.call-start = ((), (), s32[]{:S(2)}) async-start(), calls=%async_computation.6 | async-start | bytes 5242880 | tf_op jit(solution)/shard_map/all_gather | solution.py:90
  8.8 82.3 %copy-start.2 = (bf16[16,512,64]{1,2,0:T(8,128)(2,1)}, bf16[16,512,64]{1,2,0:T(8,128)(2,1)S(1)}, u32[]{:S(2)}) copy-start(bf16[16,512,64]{1,2,0:T(8,128)(2,1)S(1)} %fusion.161) | copy-start | bytes 3145732
  80.1 11.1 copy-start.24
  107.0 6.6 copy-start.19
  107.0 6.6 copy-start.6
  161.6 184.2 %reduce-scatter.6.cloned.1.call-start = ((), (), s32[]{:S(2)}) async-start(), calls=%async_computation.8 | async-start | bytes 5242880 | tf_op jit(solution)/shard_map/reduce_scatter | solution.py:97
  270.4 157.4 %all-gather.18.cloned.1.call-start = ((), (), s32[]{:S(2)}) async-start(), calls=%async_computation.9 | async-start | bytes 8650752 | tf_op jit(solution)/shard_map/all_gather | solution.py:110
  349.6 160.5 %all-gather.22.cloned.1.call-start = ((), (), s32[]{:S(2)}) async-start(), calls=%async_computation.11 | async-start | bytes 4718592 | tf_op jit(solution)/shard_map/all_gather | solution.py:114
  417.9 13.3 copy-start.25
  418.0 162.5 %all-gather.20.cloned.1.call-start = ((), (), s32[]{:S(2)}) async-start(), calls=%async_computation.10 | async-start | bytes 5242880 | tf_op jit(solution)/shard_map/all_gather | solution.py:90
  500.8 189.4 %reduce-scatter.8.cloned.1.call-start = ((), (), s32[]{:S(2)}) async-start(), calls=%async_computation.12 | async-start | bytes 5242880 | tf_op jit(solution)/shard_map/reduce_scatter | solution.py:97
  580.4 27.9 %copy-start.21 = (bf16[2,1024,1024]{2,1,0:T(8,128)(2,1)S(1)}, bf16[2,1024,1024]{2,1,0:T(8,128)(2,1)}, u32[]{:S(2)}) copy-start(bf16[2,1024,1024]{2,1,0:T(8,128)(2,1)} %all-gather.22.cloned.1.call-done) | copy-start | bytes 12582916
  614.7 77.8 %copy-start.15 = (bf16[512,1024]{1,0:T(8,128)(2,1)S(1)}, bf16[512,1024]{1,0:T(8,128)(2,1)}, u32[]{:S(2)}) copy-start(bf16[512,1024]{1,0:T(8,128)(2,1)} %param.19) | copy-start | bytes 3145732
  614.8 162.6 %all-gather.24.cloned.1.call-start = ((), (), s32[]{:S(2)}) async-start(), calls=%async_computation.13 | async-start | bytes 5242880 | tf_op jit(solution)/shard_map/all_gather | solution.py:189
  695.9 179.6 %reduce-scatter.10.cloned.1.call-start = ((), (), s32[]{:S(2)}) async-start(), calls=%async_computation.14 | async-start | bytes 5242880 | tf_op jit(solution)/shard_map/reduce_scatter | solution.py:208
  777.3 16.4 %copy-start.22 = (bf16[2,1024,1024]{2,1,0:T(8,128)(2,1)S(1)}, bf16[2,1024,1024]{2,1,0:T(8,128)(2,1)}, u32[]{:S(2)}) copy-start(bf16[2,1024,1024]{2,1,0:T(8,128)(2,1)} %all-gather.22.cloned.1.call-done) | copy-start | bytes 12582916
  800.1 240.9 %reduce-scatter.14.cloned.1.call-start = ((), (), s32[]{:S(2)}) async-start(), calls=%async_computation.16 | async-start | bytes 4718592 | tf_op jit(solution)/shard_map/reduce_scatter | solution.py:217
  800.1 8.2 copy-start.23
  800.1 8.2 copy-start.31
  815.5 575.0 %reduce-scatter.12.cloned.1.call-start = ((), (), s32[]{:S(2)}) async-start(), calls=%async_computation.15 | async-start | bytes 17301504 | tf_op jit(solution)/shard_map/reduce_scatter | solution.py:277
  880.8 6.4 copy-start.10
  1024.6 66.8 %copy-start.9 = (f32[512,1024]{1,0:T(8,128)S(1)}, f32[512,1024]{1,0:T(8,128)}, u32[]{:S(2)}) copy-start(f32[512,1024]{1,0:T(8,128)} %copy-done.8) | copy-start | bytes 6291460
  (21 other events, 59.7 us)
Sparse Core Ops, SparseCore 0:
  10.9 80.1 all-gather.11
  93.0 35.3 all-gather.15
  161.7 79.2 all-gather.13
  270.5 75.2 reduce-scatter.5
  349.7 77.9 all-gather.17
  429.7 35.3 all-gather.21
  500.9 79.4 all-gather.19
  614.9 75.2 reduce-scatter.7
  696.1 81.2 all-gather.23
  800.2 75.2 reduce-scatter.9
  879.2 51.8 reduce-scatter.13
  1024.7 365.6 reduce-scatter.11
where the time goes:
time: 1410 us; the launch traced here: 1400 us
  waiting for transfers between devices  746 us (53%)
  matrix products  314 us (22%)
  blocking collectives  214 us (15%)
  other arithmetic  59.8 us (4%)
  local copies, waits for them, and re-layouts  45.4 us (3%)
  between operations  15.8 us (1%)
    reduce_scatter x1, waiting for transfers between devices, per_device(): lax.psum_scatter(grad_attn_full, ('wide', 'narrow'), scatter_dimension=0,...  291 us
    reduce_scatter x2, waiting for transfers between devices, feed_forward(): lax.psum_scatter(lax.dot_general(active_low, w_down, contract_last, prefe...  151 us
    all_gather x2, waiting for transfers between devices, feed_forward(): ffn_rows = lax.all_gather(first_low, 'narrow', axis=0, tiled=True)  141 us
    all_gather x2, blocking collectives, run_forward(): lax.all_gather(vectors, ('wide', 'narrow'), axis=0, tiled=True)  138 us
    all_gather x1, waiting for transfers between devices, per_device(): grad_rows = lax.all_gather(grad_second_low, 'narrow', axis=0, tiled=True)  81.2 us
    dot_general x48, matrix products, masked_scores(): lax.dot_general(query_head, key_head, contract_last, preferred_element_ty...  62.4 us
    reduce_scatter x1, waiting for transfers between devices, per_device(): lax.psum_scatter(lax.dot_general(row_block, w_up, contract_last, preferre...  59.8 us
    unnamed x2, blocking collectives  57.7 us
  transfers between devices with their start and end apart: 12, of which 9 were waited for; matrix products, arithmetic and copies ran while one was open for 23% of the time, Pallas kernels for 0%

commit v1 on v0

v1 whole, which is shorter than its diff:
```python
import functools

import jax
import jax.numpy as jnp
from jax import lax
from jax.experimental import pallas as pl
from jax.experimental.pallas import tpu as pltpu
from jax.sharding import PartitionSpec as P

HEADS = 16
HEAD = 64
CHUNKS = 2
VMEM_LIMIT = 56 * 1024 * 1024

f32 = jnp.float32
bf16 = jnp.bfloat16

NT = (((1,), (1,)), ((), ()))
TN = (((0,), (0,)), ((), ()))


def dot(a, b):
    return jnp.dot(a, b, preferred_element_type=f32)


def dot_nt(a, b):
    return lax.dot_general(a, b, NT, preferred_element_type=f32)


def dot_tn(a, b):
    return lax.dot_general(a, b, TN, preferred_element_type=f32)


def swap_wide(v, mask):
    size = lax.axis_size("wide")
    return lax.ppermute(v, "wide", [(w, w ^ mask) for w in range(size)])


def shift_narrow(v, step):
    size = lax.axis_size("narrow")
    return lax.ppermute(v, "narrow", [(z, (z + step) % size) for z in range(size)])


def chip_bits():
    return (lax.axis_size("wide") // 2).bit_length() - 1


def gather_narrow(v, axis):
    size = lax.axis_size("narrow")
    pieces = [v] + [shift_narrow(v, s) for s in range(1, size)]
    return jnp.concatenate(pieces, axis)


def gather_chips(v, order):
    bits = chip_bits()
    done = []
    for bit in order:
        other = swap_wide(v, 2 << bit)
        axis = sum(1 for b in done if b > bit)
        v = jnp.stack([v, other], axis)
        done.append(bit)
    assert len(done) == bits
    return v


def bit_of(index, bit):
    return lax.rem(lax.div(index, 1 << bit), 2)


def pick(v, axis, index):
    return lax.dynamic_index_in_dim(v, index, axis, keepdims=False)


def to_slots(v, chip, core):
    bits = chip_bits()
    lead = v.shape[:-1]
    block = v.shape[-1] // lax.axis_size("wide")
    t = v.reshape(lead + (2,) * (bits + 1) + (block,))
    n = len(lead)
    for bit in range(bits):
        axis = n + bits - 1 - bit
        t = jnp.where(bit_of(chip, bit) == 1, jnp.flip(t, axis), t)
    t = jnp.where(core == 1, jnp.flip(t, n + bits), t)
    t = jnp.moveaxis(t, n + bits, n)
    return t.reshape(v.shape)


def from_slots(v, chip, core):
    bits = chip_bits()
    lead = v.shape[:-1]
    block = v.shape[-1] // lax.axis_size("wide")
    n = len(lead)
    t = v.reshape(lead + (2,) * (bits + 1) + (block,))
    t = jnp.moveaxis(t, n, n + bits)
    for bit in range(bits):
        axis = n + bits - 1 - bit
        t = jnp.where(bit_of(chip, bit) == 1, jnp.flip(t, axis), t)
    t = jnp.where(core == 1, jnp.flip(t, n + bits), t)
    return t.reshape(v.shape)


def load_rows(pos, geometry, own, other, matrix, first, count, place, sem):
    narrow, per_matrix = geometry

    def body(j, carry):
        block = matrix * per_matrix + first + j
        w = block // narrow
        z = block % narrow
        chip = (w // 2) ^ pos[0]
        core = (w % 2) ^ pos[1]
        step = lax.rem(pos[2] - z + narrow, narrow)

        @pl.when(core == 0)
        def _():
            pltpu.make_async_copy(own.at[chip, step], place(j), sem).start()

        @pl.when(core == 1)
        def _():
            pltpu.make_async_copy(other.at[chip, step], place(j), sem).start()

        return carry

    lax.fori_loop(0, count, body, 0)


def attend_forward(
    geometry, pos, x_ref, seg_row, seg_col, vec_ref, bo_ref, own_a, oth_a, own_b, oth_b,
    q_ref, k_ref, v_ref, p_ref, o_ref, h_ref, w_in, w_out, mask, sems,
):
    g = pl.program_id(0)
    steps = pl.num_programs(0)
    rows = own_a.shape[2]
    sources = ((own_a, oth_a), (own_b, oth_b))
    blocks = x_ref.shape[1] // rows

    @pl.when(g == 0)
    def _():
        for half in range(2):
            for m in range(3):
                load_rows(
                    pos, geometry, *sources[half], m, 0, blocks,
                    lambda j, half=half, m=m: w_in.at[half, m, pl.ds(pl.multiple_of(j * rows, rows), rows)],
                    sems.at[half],
                )
        for half in range(2):
            load_rows(
                pos, geometry, *sources[half], 3, 0, blocks,
                lambda j, half=half: w_out.at[half, pl.ds(pl.multiple_of(j * rows, rows), rows)],
                sems.at[2],
            )
        mask[...] = jnp.where(seg_col[...] == seg_row[...], 0.0, -1e30).astype(f32)
        pltpu.make_async_copy(w_in.at[0], w_in.at[0], sems.at[0]).wait()

    @pl.when(g == steps // 2)
    def _():
        pltpu.make_async_copy(w_in.at[1], w_in.at[1], sems.at[1]).wait()

    half = g // (steps // 2)
    columns = pl.ds(pl.multiple_of(lax.rem(g, steps // 2) * 256, 256), 256)
    x = x_ref[...]
    query = (dot(x, w_in[half, 0, :, columns]) + vec_ref[0:1, :]).astype(bf16)
    query = query * jnp.asarray(HEAD**-0.5, bf16)
    key = dot(x, w_in[half, 1, :, columns]).astype(bf16)
    value = (dot(x, w_in[half, 2, :, columns]) + vec_ref[1:2, :]).astype(bf16)
    q_ref[...] = query
    k_ref[...] = key
    v_ref[...] = value
    lane = lax.broadcasted_iota(jnp.int32, (1, 128), 1)
    for pair in range(2):
        part = slice(pair * 128, pair * 128 + 128)
        q2, k2, v2 = query[:, part], key[:, part], value[:, part]
        v2t = v2.T
        outs = []
        for sub in range(2):
            mine = (lane < HEAD) if sub == 0 else (lane >= HEAD)
            scores = dot_nt(k2, jnp.where(mine, q2, jnp.zeros_like(q2))) + mask[...]
            raised = jnp.exp(scores - jnp.max(scores, 0, keepdims=True))
            probs = (raised * (1.0 / jnp.sum(raised, 0, keepdims=True))).astype(bf16)
            p_ref[pair * 2 + sub] = probs
            outs.append(dot(v2t[sub * HEAD : sub * HEAD + HEAD], probs))
        mixed = jnp.concatenate(outs, 0).T.astype(bf16)
        o_ref[:, pl.ds(pl.multiple_of(g * 256 + pair * 128, 128), 128)] = mixed

    @pl.when(g == steps - 1)
    def _():
        pltpu.make_async_copy(w_out, w_out, sems.at[2]).wait()
        width = w_out.shape[2]
        for half in range(2):
            cols = slice(half * width, half * width + width)
            h_ref[:, cols] = (
                x_ref[:, cols].astype(f32) + dot(o_ref[...], w_out[half]) + bo_ref[0:1, cols]
            )


def run_attend_forward(pos, tokens, segment_ids, biases, own_a, oth_a, own_b, oth_b):
    count, features = tokens.shape
    rows = own_a.shape[2]
    narrow = own_a.shape[1]
    geometry = (narrow, features // rows)
    groups = features // 256
    whole = lambda *shape: pl.BlockSpec(shape, lambda g, pos: (0,) * len(shape))
    column = pl.BlockSpec((count, 256), lambda g, pos: (0, g))
    anywhere = pl.BlockSpec(memory_space=pl.ANY)
    width = features // 2
    return pl.pallas_call(
        functools.partial(attend_forward, geometry),
        grid_spec=pltpu.PrefetchScalarGridSpec(
            num_scalar_prefetch=1,
            grid=(groups,),
            in_specs=[
                whole(count, features), whole(1, count), whole(count, 1),
                pl.BlockSpec((8, 256), lambda g, pos: (0, g)), whole(8, features),
                anywhere, anywhere, anywhere, anywhere,
            ],
            out_specs=[
                column, column, column,
                pl.BlockSpec((4, count, count), lambda g, pos: (g, 0, 0)),
                whole(count, features), whole(count, features),
            ],
            scratch_shapes=[
                pltpu.VMEM((2, 3, features, width), bf16),
                pltpu.VMEM((2, features, width), bf16),
                pltpu.VMEM((count, count), f32),
                pltpu.SemaphoreType.DMA((3,)),
            ],
        ),
        out_shape=[
            jax.ShapeDtypeStruct((count, features), bf16),
            jax.ShapeDtypeStruct((count, features), bf16),
            jax.ShapeDtypeStruct((count, features), bf16),
            jax.ShapeDtypeStruct((HEADS, count, count), bf16),
            jax.ShapeDtypeStruct((count, features), bf16),
            jax.ShapeDtypeStruct((count, features), f32),
        ],
        compiler_params=pltpu.CompilerParams(
            vmem_limit_bytes=VMEM_LIMIT, dimension_semantics=("arbitrary",)
        ),
        cost_estimate=pl.CostEstimate(
            flops=2 * count * features * features * 8, bytes_accessed=24 << 20, transcendentals=0
        ),
        name="attend_forward",
    )(
        pos, tokens, segment_ids.reshape(1, count), segment_ids.reshape(count, 1),
        biases, biases[2:3] + jnp.zeros((8, 1), f32), own_a, oth_a, own_b, oth_b,
    )


def attend_backward(
    geometry, half, pos, dh_ref, add_ref, q_ref, k_ref, v_ref, p_ref, own_a, oth_a, own_b, oth_b,
    d_ref, dx_ref, bias_ref, w_in, w_out, sems,
):
    g = pl.program_id(0)
    rows = own_a.shape[2]
    features = dh_ref.shape[1]
    sources = ((own_a, oth_a), (own_b, oth_b))
    blocks = features // rows

    @pl.when(g == 0)
    def _():
        for part in range(2):
            load_rows(
                pos, geometry, *sources[part], 3, half * (blocks // 2), blocks // 2,
                lambda j, part=part: w_out.at[part, pl.ds(pl.multiple_of(j * rows, rows), rows)],
                sems.at[0],
            )
        for m in range(3):
            load_rows(
                pos, geometry, *sources[half], m, 0, blocks,
                lambda j, m=m: w_in.at[m, pl.ds(pl.multiple_of(j * rows, rows), rows)],
                sems.at[1],
            )
        pltpu.make_async_copy(w_out, w_out, sems.at[0]).wait()

    span = pl.ds(pl.multiple_of(g * 256, 256), 256)
    width = features // 2
    low = dh_ref[...].astype(bf16)
    grad_mixed = (
        dot_nt(low[:, :width], w_out[0, span, :]) + dot_nt(low[:, width:], w_out[1, span, :])
    ).astype(bf16)
    lane = lax.broadcasted_iota(jnp.int32, (1, 128), 1)
    lows = [[], [], []]
    sums = [[], []]
    for pair in range(2):
        part = slice(pair * 128, pair * 128 + 128)
        q2, k2, v2 = q_ref[:, part], k_ref[:, part], v_ref[:, part]
        do2 = grad_mixed[:, part]
        k2t = k2.T
        zero = jnp.zeros_like(q2)
        dv = dk = None
        dqs = []
        for sub in range(2):
            mine = (lane < HEAD) if sub == 0 else (lane >= HEAD)
            probs = p_ref[pair * 2 + sub]
            do_mine = jnp.where(mine, do2, zero)
            grad_probs = dot_nt(v2, do_mine)
            wide_probs = probs.astype(f32)
            inner = jnp.sum(wide_probs * grad_probs, 0, keepdims=True)
            grad_scores = (wide_probs * (grad_probs - inner)).astype(bf16)
            dv_part = dot(probs, do_mine)
            dk_part = dot(grad_scores, jnp.where(mine, q2, zero))
            dv = dv_part if dv is None else dv + dv_part
            dk = dk_part if dk is None else dk + dk_part
            dqs.append(dot(k2t[sub * HEAD : sub * HEAD + HEAD], grad_scores))
        dq = jnp.concatenate(dqs, 0).T * HEAD**-0.5
        sums[0].append(jnp.sum(dq, 0, keepdims=True))
        sums[1].append(jnp.sum(dv, 0, keepdims=True))
        for store, value in zip(lows, (dq, dk, dv)):
            store.append(value.astype(bf16))
    joined = [jnp.concatenate(s, 1) for s in lows]
    for m in range(3):
        d_ref[m] = joined[m]
    bias_ref[...] = jnp.concatenate(
        [jnp.concatenate(s, 1) for s in sums] + [jnp.zeros((6, 256), f32)], 0
    )

    @pl.when(g == 0)
    def _():
        pltpu.make_async_copy(w_in, w_in, sems.at[1]).wait()
        dx_ref[...] = add_ref[...]

    dx_ref[...] += (
        dot_nt(joined[0], w_in[0, :, span])
        + dot_nt(joined[1], w_in[1, :, span])
        + dot_nt(joined[2], w_in[2, :, span])
    )


def run_attend_backward(half, pos, grad_sum, added, q, k, v, probs, own_a, oth_a, own_b, oth_b):
    count, features = q.shape
    rows = own_a.shape[2]
    narrow = own_a.shape[1]
    geometry = (narrow, features // rows)
    groups = features // 512
    whole = lambda *shape: pl.BlockSpec(shape, lambda g, pos: (0,) * len(shape))
    column = pl.BlockSpec((count, 256), lambda g, pos: (0, half * groups + g))
    anywhere = pl.BlockSpec(memory_space=pl.ANY)
    width = features // 2
    return pl.pallas_call(
        functools.partial(attend_backward, geometry, half),
        grid_spec=pltpu.PrefetchScalarGridSpec(
            num_scalar_prefetch=1,
            grid=(groups,),
            in_specs=[
                whole(count, features), whole(count, features), column, column, column,
                pl.BlockSpec((4, count, count), lambda g, pos: (half * groups + g, 0, 0)),
                anywhere, anywhere, anywhere, anywhere,
            ],
            out_specs=[
                pl.BlockSpec((3, count, 256), lambda g, pos: (0, 0, g)),
                whole(count, features),
                pl.BlockSpec((8, 256), lambda g, pos: (0, g)),
            ],
            scratch_shapes=[
                pltpu.VMEM((3, features, width), bf16),
                pltpu.VMEM((2, width, width), bf16),
                pltpu.SemaphoreType.DMA((2,)),
            ],
        ),
        out_shape=[
            jax.ShapeDtypeStruct((3, count, width), bf16),
            jax.ShapeDtypeStruct((count, features), f32),
            jax.ShapeDtypeStruct((8, width), f32),
        ],
        compiler_params=pltpu.CompilerParams(
            vmem_limit_bytes=VMEM_LIMIT, dimension_semantics=("arbitrary",)
        ),
        cost_estimate=pl.CostEstimate(
            flops=2 * count * features * features * 6, bytes_accessed=16 << 20, transcendentals=0
        ),
        name="attend_backward",
    )(pos, grad_sum, added, q, k, v, probs, own_a, oth_a, own_b, oth_b)


def moments(hidden):
    center = hidden - jnp.mean(hidden, -1, keepdims=True)
    return center, lax.rsqrt(jnp.mean(center * center, -1, keepdims=True) + 1e-12)


def norm_back(grad, normed, factor):
    return factor * (
        grad
        - jnp.mean(grad, -1, keepdims=True)
        - normed * jnp.mean(grad * normed, -1, keepdims=True)
    )


def gelu_pair(a):
    z = jnp.abs(a) * (0.5**0.5)
    t = 1.0 / (1.0 + 0.3275911 * z)
    poly = t * (
        0.127414796 + t * (-0.142248368 + t * (0.7107068705 + t * (-0.7265760135 + t * 0.5307027145)))
    )
    bell = jnp.exp(-0.5 * (a * a))
    tail = poly * bell
    phi = jnp.where(a >= 0, 1.0 - tail, tail)
    return a * phi, phi + a * (bell * 0.3989422804014327)


ROWS_AT_ONCE = 128


def row_blocks(count):
    return [slice(r, r + ROWS_AT_ONCE) for r in range(0, count, ROWS_AT_ONCE)]


def ffn_forward(first, last, *refs):
    refs = list(refs)
    h_ref, vec, w1a, w1b, w2a, w2b, b1 = refs[:7]
    refs = refs[7:]
    f_in = None if first else refs.pop(0)
    dy = refs.pop(0) if last else None
    act_ref, slope_ref = refs[:2]
    refs = refs[2:]
    u_out = refs.pop(0) if first else None
    if last:
        result, dh, dh_low, sums = refs[:4]
        refs = refs[4:]
        total, u_low = refs
    else:
        total, u_low = refs
    t = pl.program_id(0)
    count, features = h_ref.shape
    width = features // 2

    @pl.when(t == 0)
    def _():
        for r in row_blocks(count):
            center, factor = moments(h_ref[r, :])
            u_low[r, :] = (center * factor * (1.0 + vec[0:1, :]) + vec[1:2, :]).astype(bf16)
        if first:
            u_out[...] = u_low[...]
            total[...] = jnp.zeros_like(total)
        else:
            total[...] = f_in[...]

    a = dot(u_low[:, :width], w1a[...]) + dot(u_low[:, width:], w1b[...]) + b1[0:1, :]
    act, slope = gelu_pair(a)
    act = act.astype(bf16)
    act_ref[...] = act
    slope_ref[...] = slope.astype(bf16)
    total[:, :width] += dot_nt(act, w2a[...])
    total[:, width:] += dot_nt(act, w2b[...])
    if last:

        @pl.when(t == pl.num_programs(0) - 1)
        def _():
            sums[...] = jnp.zeros_like(sums)
            for r in row_blocks(count):
                center, factor = moments(h_ref[r, :])
                u = center * factor * (1.0 + vec[0:1, :]) + vec[1:2, :]
                center, factor = moments(u + total[r, :] + vec[2:3, :])
                normed = center * factor
                result[r, :] = (normed * (1.0 + vec[3:4, :]) + vec[4:5, :]).astype(bf16)
                grad = dy[r, :].astype(f32)
                back = norm_back(grad * (1.0 + vec[3:4, :]), normed, factor)
                dh[r, :] = back
                dh_low[r, :] = back.astype(bf16)
                sums[0:1, :] += jnp.sum(grad, 0, keepdims=True)
                sums[1:2, :] += jnp.sum(grad * normed, 0, keepdims=True)
                sums[2:3, :] += jnp.sum(back, 0, keepdims=True)


TILE = 512


def run_ffn_forward(hidden, vec, w1, w2, b1, earlier, dy):
    count, features = hidden.shape
    width, units = w1[0].shape
    first, last = earlier is None, dy is not None
    whole = lambda *shape: pl.BlockSpec(shape, lambda t: (0,) * len(shape))
    tall = pl.BlockSpec((width, TILE), lambda t: (0, t))
    strip = pl.BlockSpec((count, TILE), lambda t: (0, t))
    ins = [hidden, vec, w1[0], w1[1], w2[0], w2[1], b1]
    in_specs = [
        whole(count, features), whole(8, features), tall, tall, tall, tall,
        pl.BlockSpec((1, TILE), lambda t: (0, t)),
    ]
    out_specs = [strip, strip]
    out_shape = [jax.ShapeDtypeStruct((count, units), bf16)] * 2
    scratch = [pltpu.VMEM((count, features), bf16)]
    if not first:
        ins.append(earlier)
        in_specs.append(whole(count, features))
    if last:
        ins.append(dy)
        in_specs.append(whole(count, features))
    if first:
        out_specs.append(whole(count, features))
        out_shape.append(jax.ShapeDtypeStruct((count, features), bf16))
    if last:
        out_specs += [whole(count, features)] * 3 + [whole(8, features)]
        out_shape += [
            jax.ShapeDtypeStruct((count, features), bf16),
            jax.ShapeDtypeStruct((count, features), f32),
            jax.ShapeDtypeStruct((count, features), bf16),
            jax.ShapeDtypeStruct((8, features), f32),
        ]
        scratch = [pltpu.VMEM((count, features), f32)] + scratch
    else:
        out_specs.append(whole(count, features))
        out_shape.append(jax.ShapeDtypeStruct((count, features), f32))
    return pl.pallas_call(
        functools.partial(ffn_forward, first, last),
        grid=(units // TILE,),
        in_specs=in_specs,
        out_specs=out_specs,
        out_shape=out_shape,
        scratch_shapes=scratch,
        compiler_params=pltpu.CompilerParams(
            vmem_limit_bytes=VMEM_LIMIT, dimension_semantics=("arbitrary",)
        ),
        cost_estimate=pl.CostEstimate(
            flops=4 * count * features * units * 2, bytes_accessed=16 << 20, transcendentals=0
        ),
        name="ffn_forward",
    )(*ins)


def ffn_backward(first, last, *refs):
    refs = list(refs)
    dh_low, w1a, w1b, w2a, w2b, slope = refs[:6]
    refs = refs[6:]
    du_in = None if first else refs.pop(0)
    if last:
        dh, h_ref, vec = refs[:3]
        refs = refs[3:]
    da_ref, db_ref = refs[:2]
    refs = refs[2:]
    if last:
        dh1, sums, total = refs
    else:
        (total,) = refs
    t = pl.program_id(0)
    count, features = dh_low.shape
    width = features // 2

    @pl.when(t == 0)
    def _():
        total[...] = jnp.zeros_like(total) if first else du_in[...]

    grad = dot(dh_low[:, :width], w2a[...]) + dot(dh_low[:, width:], w2b[...])
    grad = grad * slope[...].astype(f32)
    db_ref[...] = jnp.sum(grad, 0, keepdims=True)
    low = grad.astype(bf16)
    da_ref[...] = low
    total[:, :width] += dot_nt(low, w1a[...])
    total[:, width:] += dot_nt(low, w1b[...])
    if last:

        @pl.when(t == pl.num_programs(0) - 1)
        def _():
            sums[...] = jnp.zeros_like(sums)
            for r in row_blocks(count):
                center, factor = moments(h_ref[r, :])
                normed = center * factor
                du = total[r, :] + dh[r, :]
                back = norm_back(du * (1.0 + vec[0:1, :]), normed, factor)
                dh1[r, :] = back
                sums[0:1, :] += jnp.sum(du, 0, keepdims=True)
                sums[1:2, :] += jnp.sum(du * normed, 0, keepdims=True)
                sums[2:3, :] += jnp.sum(back, 0, keepdims=True)


def run_ffn_backward(dh_low, w1, w2, slope, earlier, tail):
    count, features = dh_low.shape
    width, units = w1[0].shape
    first, last = earlier is None, tail is not None
    whole = lambda *shape: pl.BlockSpec(shape, lambda t: (0,) * len(shape))
    tall = pl.BlockSpec((width, TILE), lambda t: (0, t))
    strip = pl.BlockSpec((count, TILE), lambda t: (0, t))
    ins = [dh_low, w1[0], w1[1], w2[0], w2[1], slope]
    in_specs = [whole(count, features), tall, tall, tall, tall, strip]
    out_specs = [strip, pl.BlockSpec((1, TILE), lambda t: (0, t))]
    out_shape = [
        jax.ShapeDtypeStruct((count, units), bf16),
        jax.ShapeDtypeStruct((1, units), f32),
    ]
    scratch = []
    if not first:
        ins.append(earlier)
        in_specs.append(whole(count, features))
    if last:
        ins += list(tail)
        in_specs += [whole(count, features), whole(count, features), whole(8, features)]
        out_specs += [whole(count, features), whole(8, features)]
        out_shape += [
            jax.ShapeDtypeStruct((count, features), f32),
            jax.ShapeDtypeStruct((8, features), f32),
        ]
        scratch = [pltpu.VMEM((count, features), f32)]
    else:
        out_specs.append(whole(count, features))
        out_shape.append(jax.ShapeDtypeStruct((count, features), f32))
    return pl.pallas_call(
        functools.partial(ffn_backward, first, last),
        grid=(units // TILE,),
        in_specs=in_specs,
        out_specs=out_specs,
        out_shape=out_shape,
        scratch_shapes=scratch,
        compiler_params=pltpu.CompilerParams(
            vmem_limit_bytes=VMEM_LIMIT, dimension_semantics=("arbitrary",)
        ),
        cost_estimate=pl.CostEstimate(
            flops=4 * count * features * units * 2, bytes_accessed=16 << 20, transcendentals=0
        ),
        name="ffn_backward",
    )(*ins)


def add_low(a, b):
    return (a.astype(f32) + b.astype(f32)).astype(bf16)


def scatter_ffn(own, other, order):
    bits = chip_bits()
    narrow = lax.axis_size("narrow")
    received = swap_wide(other().astype(bf16), 1)
    part = (own() + received.astype(f32)).astype(bf16)
    rows, columns = part.shape
    part = part.reshape((2,) * bits + (rows >> bits, columns))
    left = list(range(bits - 1, -1, -1))
    for bit in order:
        axis = left.index(bit)
        received = swap_wide(lax.index_in_dim(part, 1, axis, keepdims=False), 2 << bit)
        part = add_low(lax.index_in_dim(part, 0, axis, keepdims=False), received)
        left.remove(bit)
    part = part.reshape(rows >> bits, narrow, columns // narrow)
    total = part[:, 0].astype(f32)
    for s in range(1, narrow):
        total = total + shift_narrow(part[:, narrow - s], s).astype(f32)
    return total


def scatter_attn(own, other, order, chip, z, rows_each):
    bits = chip_bits()
    narrow = lax.axis_size("narrow")
    received = swap_wide(other().astype(bf16), 1)
    part = (own() + received.astype(f32)).astype(bf16)
    low_bits = bits - 2
    columns = part.shape[1] // 4
    part = part.reshape((2,) * low_bits + (narrow * rows_each, 2, 2, columns))
    names = list(range(low_bits - 1, -1, -1)) + [None, bits - 1, bits - 2, None]
    for bit in order:
        axis = names.index(bit)
        mine = bit_of(chip, bit)
        received = swap_wide(pick(part, axis, 1 - mine), 2 << bit)
        part = add_low(pick(part, axis, mine), received)
        names.pop(axis)
    part = part.reshape(narrow, rows_each, columns)
    total = pick(part, 0, z).astype(f32)
    for s in range(1, narrow):
        total = total + shift_narrow(pick(part, 0, lax.rem(z + s, narrow)), s).astype(f32)
    return total


def per_device(tokens, segment_ids, attn_weight, vectors, ffn_weight, ffn_bias, out_grad):
    wide, narrow = lax.axis_size("wide"), lax.axis_size("narrow")
    w, z = lax.axis_index("wide"), lax.axis_index("narrow")
    chip, core = lax.div(w, 2), lax.rem(w, 2)
    bits = chip_bits()
    up = list(range(bits))
    down = up[::-1]
    pos = jnp.stack([chip, core, z]).astype(jnp.int32)
    count, features = tokens.shape
    half = features // 2

    each, each_bias = vectors.shape[0], ffn_bias.shape[0]
    room = -(-(each + each_bias) // 128) * 128
    small = jnp.concatenate(
        [vectors, ffn_bias, jnp.zeros((room - each - each_bias,), bf16)]
    ).reshape(1, room)
    small = gather_narrow(small, 0)
    small = gather_chips(small, up).reshape(-1, room)
    small = jnp.concatenate([small, swap_wide(small, 1)], 0)
    slots = jnp.arange(wide * narrow)
    slot_core, slot_chip, slot_z = (
        slots // (wide * narrow // 2), (slots // narrow) % (wide // 2), slots % narrow,
    )
    slot_w = (slot_chip ^ chip) * 2 + (slot_core ^ core)
    whole_at = slot_w * narrow + lax.rem(z - slot_z + narrow, narrow)
    bias_at = slot_z * wide + slot_w
    spots = jnp.arange(wide * narrow)[:, None]
    vec_rows = dot((spots == whole_at[None, :]).astype(bf16), small[:, :each]).reshape(8, features)
    bias_rel = dot(
        (spots == bias_at[None, :]).astype(bf16), small[:, each : each + each_bias]
    ).reshape(narrow, CHUNKS, -1)
    bq, bv, bo, s1, bf, s2, g1, g2 = [vec_rows[i] for i in range(8)]
    slot_vec = to_slots(jnp.stack([g1, s1, bf, g2, s2, s2, s2, s2]), chip, core)
    dy = to_slots(out_grad, chip, core)

    rows_each = attn_weight.shape[0]
    halves = []
    for part, order in ((0, up), (1, down)):
        v = attn_weight[:, part * half : part * half + half].reshape(1, rows_each, half)
        v = gather_narrow(v, 0)
        v = gather_chips(v, order).reshape(wide // 2, narrow, rows_each, half)
        halves += [v, swap_wide(v, 1)]

    units = ffn_weight.shape[2] // CHUNKS
    ffn = []
    for c in range(CHUNKS):
        pair = []
        for which, order in ((0, up), (1, down)):
            v = ffn_weight[which, :, c * units : c * units + units]
            v = gather_narrow(v, 1)
            v = gather_chips(v, order).reshape(-1, narrow * units)
            pair.append((v, swap_wide(v, 1)))
        ffn.append(pair)

    biases = jnp.stack([bq, bv, bo, bo, bo, bo, bo, bo])
    q, k, v, probs, mixed, hidden = run_attend_forward(pos, tokens, segment_ids, biases, *halves)
    hidden = to_slots(hidden, chip, core)
    acts, slopes = [], []
    total = None
    for c in range(CHUNKS):
        b1 = bias_rel[:, c].reshape(1, -1)
        outs = run_ffn_forward(
            hidden, slot_vec, *ffn[c], b1, total, dy if c == CHUNKS - 1 else None
        )
        acts.append(outs[0])
        slopes.append(outs[1])
        rest = outs[2:]
        if c == 0:
            u_low = rest[0]
            rest = rest[1:]
        if c < CHUNKS - 1:
            total = rest[0]
    result, dh, dh_low, sums_two = rest
    result = from_slots(result, chip, core)

    grad_down = [
        scatter_ffn(
            functools.partial(dot_tn, dh_low[:, :half], acts[c]),
            functools.partial(dot_tn, dh_low[:, half:], acts[c]),
            down,
        )
        for c in range(CHUNKS)
    ]
    total = None
    das, dbs = [], []
    for c in range(CHUNKS):
        outs = run_ffn_backward(
            dh_low, *ffn[c], slopes[c], total, (dh, hidden, slot_vec) if c == CHUNKS - 1 else None
        )
        das.append(outs[0])
        dbs.append(outs[1])
        total = outs[2]
    grad_sum, sums_one = total, outs[3]
    grad_up = [
        scatter_ffn(
            functools.partial(dot_tn, u_low[:, :half], das[c]),
            functools.partial(dot_tn, u_low[:, half:], das[c]),
            up,
        )
        for c in range(CHUNKS)
    ]
    grad_ffn = jnp.stack(
        [jnp.concatenate(grad_up, -1), jnp.concatenate(grad_down, -1)]
    )

    grad_sum = from_slots(grad_sum, chip, core)
    grad_low = grad_sum.astype(bf16)

    def core_columns(v, which):
        t = v.reshape(count, -1, 2, narrow * rows_each)
        return pick(t, 2, which).reshape(count, half)

    x_own, x_oth = core_columns(tokens, core), core_columns(tokens, 1 - core)
    o_own, o_oth = core_columns(mixed, core), core_columns(mixed, 1 - core)
    grad_tokens = grad_sum
    grad_attn, bias_sums = [], []
    for part, order in ((0, down), (1, up)):
        grads, grad_tokens, bias_sum = run_attend_backward(
            part, pos, grad_sum, grad_tokens, q, k, v, probs, *halves
        )
        bias_sums.append(bias_sum)
        columns = slice(part * half, part * half + half)

        def weights(x_rows, o_rows, grads=grads, columns=columns):
            return jnp.concatenate(
                [dot_tn(x_rows, grads[m]) for m in range(3)]
                + [dot_tn(o_rows, grad_low[:, columns])],
                1,
            )

        grad_attn.append(
            scatter_attn(
                functools.partial(weights, x_own, o_own),
                functools.partial(weights, x_oth, o_oth),
                order, chip, z, rows_each,
            )
        )
    grad_attn = jnp.concatenate(grad_attn, 1)

    slot_sums = from_slots(jnp.concatenate([sums_one[:3], sums_two[:3]]), chip, core)
    gs1, gg1, gbo, gs2, gg2, gbf = [slot_sums[i] for i in range(6)]
    gbq = jnp.concatenate([bias_sums[0][0], bias_sums[1][0]])
    gbv = jnp.concatenate([bias_sums[0][1], bias_sums[1][1]])
    vec = jnp.concatenate([gbq, gbv, gbo, gs1, gbf, gs2, gg1, gg2]).reshape(wide, narrow, each)
    db = jnp.stack([d.reshape(narrow, -1) for d in dbs], 1).reshape(narrow, wide, each_bias)
    part = jnp.concatenate([vec, db.transpose(1, 0, 2)], 2)
    part = part.reshape((2,) * (bits + 1) + part.shape[1:])
    for bit in range(bits + 1):
        axis = bits - bit
        mine = bit_of(w, bit)
        part = pick(part, axis, mine) + swap_wide(pick(part, axis, 1 - mine), 1 << bit)
    at = lambda s: jnp.concatenate(
        [pick(part[:, :each], 0, lax.rem(z + s, narrow)), part[(narrow - s) % narrow, each:]]
    )
    tally = at(0)
    for s in range(1, narrow):
        tally = tally + shift_narrow(at(s), s)
    return (result, grad_tokens, grad_attn, tally[:each], grad_ffn, tally[each:])


def solution(mesh):
    return jax.shard_map(
        per_device,
        mesh=mesh,
        in_specs=(
            P(("wide", "narrow"), None),
            P(("wide", "narrow"), None),
            P(("wide", "narrow"), None),
            P(("wide", "narrow")),
            P(None, "wide", "narrow"),
            P(("narrow", "wide")),
            P(("wide", "narrow"), None),
        ),
        out_specs=(
            P(("wide", "narrow"), None),
            P(("wide", "narrow"), None),
            P(("wide", "narrow"), None),
            P(("wide", "narrow")),
            P(None, "wide", "narrow"),
            P(("narrow", "wide")),
        ),
        check_vma=False,
    )
```

time: 1410 us -> 628 us (0.45)
  waiting for transfers between devices: 746 us -> 152 us
  matrix products: 314 us -> 51.4 us
  blocking collectives: 214 us -> 0 us
  starting transfers between devices: 1.09 us -> 123 us
  Pallas kernels: 0 us -> 117 us
  local copies, waits for them, and re-layouts: 45.4 us -> 105 us
    reduce_scatter x5 -> x0, waiting for transfers between devices: 501 us -> none  [the longest x1 291 us: per_device(): lax.psum_scatter(grad_attn_full, ('wide', 'narrow'), scatter_dimension=0,...]
    dot_general x159 -> x26, matrix products: 314 us -> 51.4 us  [the longest x24 50.4 us: dot_tn(): return lax.dot_general(a, b, TN, preferred_element_type=f32)]
    all_gather x7 -> x0, waiting for transfers between devices: 243 us -> none  [the longest x2 141 us: feed_forward(): ffn_rows = lax.all_gather(first_low, 'narrow', axis=0, tiled=True)]
    all_gather x4 -> x0, blocking collectives: 156 us -> none  [the longest x2 138 us: run_forward(): lax.all_gather(vectors, ('wide', 'narrow'), axis=0, tiled=True)]
    ppermute x0 -> x84, waiting for transfers between devices: none -> 152 us  [the longest x42 120 us: swap_wide(): return lax.ppermute(v, 'wide', [(w, w ^ mask) for w in range(size)])]
    ppermute x0 -> x84, starting transfers between devices: none -> 123 us  [the longest x42 84.7 us: shift_narrow(): lax.ppermute(v, 'narrow', [(z, (z + step) % size) for z in range(size)])]
    pallas_call x0 -> x7, Pallas kernels: none -> 117 us  [the longest x2 38.9 us: run_ffn_forward(): pl.pallas_call(functools.partial(ffn_forward, first, last), grid=(units /...]
    unnamed x2 -> x0, blocking collectives: 57.7 us -> none
  transfers between devices with their start and end apart: 12 -> 84, of which waited for: 9 -> 27; matrix products, arithmetic and copies ran while one was open for 23% -> 27% of each run, Pallas kernels for 0% -> 7%
where the time goes in v1:
time: 628 us; the launch traced here: 619 us
  waiting for transfers between devices  152 us (24%)
  starting transfers between devices  123 us (20%)
  Pallas kernels  117 us (19%)
  local copies, waits for them, and re-layouts  105 us (17%)
  other arithmetic  68.1 us (11%)
  matrix products  51.4 us (8%)
    ppermute x42, waiting for transfers between devices, swap_wide(): return lax.ppermute(v, 'wide', [(w, w ^ mask) for w in range(size)])  120 us
    ppermute x42, starting transfers between devices, shift_narrow(): lax.ppermute(v, 'narrow', [(z, (z + step) % size) for z in range(size)])  84.7 us
    dot_general x24, matrix products, dot_tn(): return lax.dot_general(a, b, TN, preferred_element_type=f32)  50.4 us
    pallas_call x2, Pallas kernels, run_ffn_forward(): pl.pallas_call(functools.partial(ffn_forward, first, last), grid=(units /...  38.9 us
    ppermute x42, starting transfers between devices, swap_wide(): return lax.ppermute(v, 'wide', [(w, w ^ mask) for w in range(size)])  37.9 us
    pallas_call x2, Pallas kernels, run_attend_backward(): pl.pallas_call(functools.partial(attend_backward, geometry, half), grid_s...  33.9 us
    ppermute x42, waiting for transfers between devices, shift_narrow(): lax.ppermute(v, 'narrow', [(z, (z + step) % size) for z in range(size)])  31.5 us
    pallas_call x2, Pallas kernels, run_ffn_backward(): pl.pallas_call(functools.partial(ffn_backward, first, last), grid=(units...  23 us
  transfers between devices with their start and end apart: 84, of which 27 were waited for; matrix products, arithmetic and copies ran while one was open for 27% of the time, Pallas kernels for 7%

profile of v1, /device:TPU:0, one launch (start us, length us, event | category | flops | bytes accessed | tf_op | source)
XLA Modules:
  0.0 618.5 jit_solution(268342487449822480)
XLA Ops:
  15.3 5.5 rev.74
  53.2 7.8 %collective-permute-start.30 = (bf16[128,512]{1,0:T(8,128)(2,1)S(1)}, bf16[128,512]{1,0:T(8,128)(2,1)S(1)}, u32[]{:S(2)}, u32[]{:S(2)}) collective-permute-start(bf16[128,512]{1,0:T(8,128)(2,1)S(1)} %copy-done.27), channel_id=1, source_target_pairs={{0,1},{1,2},{2,3},{3,0},{4,5},{5,6},{6,7},{7,4},{8,9},{9,10},{10,1... | collective-permute-start | bytes 393224 | tf_op jit(solution)/shard_map/ppermute | solution.py:41
  65.8 5.2 collective-permute-start.25
  90.7 4.7 collective-permute-done.19
  102.9 14.6 %collective-permute-done.10 = bf16[2,4,128,512]{3,2,1,0:T(8,128)(2,1)S(1)} collective-permute-done((bf16[2,4,128,512]{3,2,1,0:T(8,128)(2,1)S(1)}, bf16[2,4,128,512]{3,2,1,0:T(8,128)(2,1)S(1)}, u32[]{:S(2)}, u32[]{:S(2)}) %collective-permute-start.10) | collective-permute-done | bytes 1048608 | tf_op jit(solution)/shard_map/ppermute | solution.py:36
  120.9 5.4 collective-permute-done.27
  133.5 10.5 %collective-permute-done.40 = bf16[2,128,2048]{2,1,0:T(8,128)(2,1)} collective-permute-done((bf16[2,128,2048]{2,1,0:T(8,128)(2,1)}, bf16[2,128,2048]{2,1,0:T(8,128)(2,1)}, u32[]{:S(2)}, u32[]{:S(2)}) %collective-permute-start.40) | collective-permute-done | bytes 1048608 | tf_op jit(solution)/shard_map/ppermute | solution.py:36
  147.7 5.0 collective-permute-done.34
  162.8 9.2 %collective-permute-done.22 = bf16[2,128,2048]{2,1,0:T(8,128)(2,1)S(1)} collective-permute-done((bf16[2,128,2048]{2,1,0:T(8,128)(2,1)S(1)}, bf16[2,128,2048]{2,1,0:T(8,128)(2,1)S(1)}, u32[]{:S(2)}, u32[]{:S(2)}) %collective-permute-start.22) | collective-permute-done | bytes 1048608 | tf_op jit(solution)/shard_map/ppermute | solution.py:36
  174.7 21.5 %attend_forward.1 = (bf16[512,1024]{1,0:T(8,128)(2,1)}, bf16[512,1024]{1,0:T(8,128)(2,1)}, bf16[512,1024]{1,0:T(8,128)(2,1)}, bf16[16,512,512]{2,1,0:T(8,128)(2,...) custom-call(s32[3]{0:T(128)} %pad_add_fusion.pos, bf16[512,1024]{1,0:T(8,128)(2,1)} %x_ref.1, s32[1,512]{1,0:T(1,128)} %seg_row.1, ...), custom_call_target="tpu_custom_call" | custom-call | flops 8589934592 | bytes 25165824 | tf_op jit(solution)/shard_map/attend_forward/pallas_call | solution.py:205
  205.9 10.9 %rev.68 = f32[512,2,2,2,128]{4,3,2,1,0:T(2,128)} reverse(f32[512,2,2,2,128]{4,3,2,1,0:T(2,128)} %reverse_select_fusion.2), dimensions={3} | reverse | bytes 4194304 | tf_op jit(solution)/shard_map/jit(_flip)/rev | solution.py:83
  222.0 21.6 %ffn_forward.2 = (bf16[512,2048]{1,0:T(8,128)(2,1)}, bf16[512,2048]{1,0:T(8,128)(2,1)}, bf16[512,1024]{1,0:T(8,128)(2,1)}, f32[512,1024]{1,0:T(8,128)}) custom-call(f32[512,1024]{1,0:T(8,128)} %reshape.291.refs_0_.refs_8_, f32[8,1024]{1,0:T(8,128)} %bitcast.431, bf16[512,2048]{1,0:T(8,128)(2,1)} %bitcast.49.refs_2_.refs_1_, ...), custom_call_target="tpu_custom_call" | custom-call | flops 8589934592 | bytes 16777216 | tf_op jit(solution)/shard_map/ffn_forward/pallas_call | solution.py:502
  243.7 17.3 %ffn_forward.3 = (bf16[512,2048]{1,0:T(8,128)(2,1)}, bf16[512,2048]{1,0:T(8,128)(2,1)}, bf16[512,1024]{1,0:T(8,128)(2,1)}, f32[512,1024]{1,0:T(8,128)}, bf16[512,1024]{1,0:T(8,128)(2,1)}, /*index=5*/f32[8,1024]{1,0:T(8,128)}) custom-call(f32[512,1024]{1,0:T(8,128)} %reshape.291.refs_0_.refs_8_, f32[8,1024]{1,0:T(8,128)} %bitcast.432, ...), custom_call_target="tpu_custom_call" | custom-call | flops 8589934592 | bytes 16777216 | tf_op jit(solution)/shard_map/ffn_forward/pallas_call | solution.py:502
  261.0 9.6 %ffn_backward.2 = (bf16[512,2048]{1,0:T(8,128)(2,1)}, f32[1,2048]{1,0:T(1,128)}, f32[512,1024]{1,0:T(8,128)}) custom-call(bf16[512,1024]{1,0:T(8,128)(2,1)} %get-tuple-element.38.refs_0_, bf16[512,2048]{1,0:T(8,128)(2,1)} %bitcast.49.refs_2_.refs_1_, bf16[512,2048]{1,0:T(8,128)(2,1)} %collective-permute-done.35.refs_3_.refs_2_, ...), custom_call_target="tpu_custom_call" | custom-call | flops 8589934592 | bytes 16777216 | tf_op jit(solution)/shard_map/ffn_backward/pallas_call | solution.py:594
  270.6 13.4 %ffn_backward.3 = (bf16[512,2048]{1,0:T(8,128)(2,1)}, f32[1,2048]{1,0:T(1,128)}, f32[512,1024]{1,0:T(8,128)}, f32[8,1024]{1,0:T(8,128)}) custom-call(bf16[512,1024]{1,0:T(8,128)(2,1)} %get-tuple-element.38.refs_0_, bf16[512,2048]{1,0:T(8,128)(2,1)} %bitcast.36.refs_2_.refs_1_, bf16[512,2048]{1,0:T(8,128)(2,1)} %collective-permute-done.23.refs_3_.refs_2_, ...), custom_call_target="tpu_custom_call" | custom-call | flops 8589934592 | bytes 16777216 | tf_op jit(solution)/shard_map/ffn_backward/pallas_call | solution.py:594
  291.8 10.9 %rev.80 = f32[512,2,2,2,128]{4,3,2,1,0:T(2,128)} reverse(f32[512,2,2,2,128]{4,3,2,1,0:T(2,128)} %reverse_select_fusion), dimensions={3} | reverse | bytes 4194304 | tf_op jit(solution)/shard_map/jit(_flip)/rev | solution.py:98
  310.1 17.3 %attend_backward.2 = (bf16[3,512,512]{2,1,0:T(8,128)(2,1)}, f32[512,1024]{1,0:T(8,128)}, f32[8,512]{1,0:T(8,128)}) custom-call(s32[3]{0:T(128)} %pad_add_fusion.pos, f32[512,1024]{1,0:T(8,128)} %copy-done, f32[512,1024]{1,0:T(8,128)} %copy-done, bf16[512,1024]{1,0:T(8,128)(2,1)} %get-tuple-element.44.q_ref, bf16[512,1024]{1,0:T(8,128)(2,1)} %get-tuple-element.45.k_ref, ...), custom_call_target="tpu_custom_call" | custom-call | flops 6442450944 | bytes 16777216 | tf_op jit(solution)/shard_map/attend_backward/pallas_call | solution.py:338
  342.0 16.7 %attend_backward.3 = (bf16[3,512,512]{2,1,0:T(8,128)(2,1)}, f32[512,1024]{1,0:T(8,128)}, f32[8,512]{1,0:T(8,128)}) custom-call(s32[3]{0:T(128)} %pad_add_fusion.pos, f32[512,1024]{1,0:T(8,128)} %copy-done, f32[512,1024]{1,0:T(8,128)} %get-tuple-element.48.add_ref, bf16[512,1024]{1,0:T(8,128)(2,1)} %get-tuple-element.44.q_ref, ...), custom_call_target="tpu_custom_call" | custom-call | flops 6442450944 | bytes 16777216 | tf_op jit(solution)/shard_map/attend_backward/pallas_call | solution.py:338
  389.8 7.8 %rev.77 = bf16[512,2,2,2,128]{4,3,2,1,0:T(2,128)(2,1)} reverse(bf16[512,2,2,2,128]{4,3,2,1,0:T(2,128)(2,1)S(1)} %broadcast_select_fusion.2), dimensions={3} | reverse | bytes 2097152 | tf_op jit(solution)/shard_map/jit(_flip)/rev | solution.py:98
  470.6 6.8 %collective-permute-done.67 = bf16[2,128,2048]{1,2,0:T(8,128)(2,1)} collective-permute-done((bf16[2,128,2048]{1,2,0:T(8,128)(2,1)}, bf16[2,128,2048]{1,2,0:T(8,128)(2,1)}, u32[]{:S(2)}, u32[]{:S(2)}) %collective-permute-start.67) | collective-permute-done | bytes 1048608 | tf_op jit(solution)/shard_map/ppermute | solution.py:36
  484.6 20.0 %collective-permute-done.79 = bf16[2,128,2048]{1,2,0:T(8,128)(2,1)} collective-permute-done((bf16[2,128,2048]{1,2,0:T(8,128)(2,1)}, bf16[2,128,2048]{1,2,0:T(8,128)(2,1)}, u32[]{:S(2)}, u32[]{:S(2)}) %collective-permute-start.79) | collective-permute-done | bytes 1048608 | tf_op jit(solution)/shard_map/ppermute | solution.py:36
  507.1 20.0 %collective-permute-done.43 = bf16[512,2,512]{0,2,1:T(8,128)(2,1)S(1)} collective-permute-done((bf16[512,2,512]{0,2,1:T(8,128)(2,1)S(1)}, bf16[512,2,512]{0,2,1:T(8,128)(2,1)S(1)}, u32[]{:S(2)}, u32[]{:S(2)}) %collective-permute-start.43) | collective-permute-done | bytes 1048608 | tf_op jit(solution)/shard_map/ppermute | solution.py:36
  530.6 7.6 %collective-permute-done.62 = bf16[128,2048]{0,1:T(8,128)(2,1)S(1)} collective-permute-done((bf16[128,2048]{0,1:T(8,128)(2,1)S(1)}, bf16[128,2048]{0,1:T(8,128)(2,1)S(1)}, u32[]{:S(2)}, u32[]{:S(2)}) %collective-permute-start.62) | collective-permute-done | bytes 524320 | tf_op jit(solution)/shard_map/ppermute | solution.py:36
  540.1 9.4 %collective-permute-done.68 = bf16[128,2048]{0,1:T(8,128)(2,1)S(1)} collective-permute-done((bf16[128,2048]{0,1:T(8,128)(2,1)S(1)}, bf16[128,2048]{0,1:T(8,128)(2,1)S(1)}, u32[]{:S(2)}, u32[]{:S(2)}) %collective-permute-start.68) | collective-permute-done | bytes 524320 | tf_op jit(solution)/shard_map/ppermute | solution.py:36
  (463 shorter events, 337.3 us)
Async XLA Ops:
  9.4 31.4 %collective-permute-start.12 = (bf16[1,128,512]{2,1,0:T(8,128)(2,1)S(1)}, bf16[1,128,512]{2,1,0:T(8,128)(2,1)}, u32[]{:S(2)}, u32[]{:S(2)}) collective-permute-start(bf16[1,128,512]{2,1,0:T(8,128)(2,1)S(1)} %get-tuple-element.132), channel_id=1, source_target_pairs={{0,1},{1,2},{2,3},{3,0},{4,5},{5,6},{6,7},{7,4},{8,9},{9,10},{10,1... | collective-permute-start | bytes 393224 | tf_op jit(solution)/shard_map/ppermute | solution.py:41
  10.1 33.7 %collective-permute-start.13 = (bf16[1,128,512]{2,1,0:T(8,128)(2,1)S(1)}, bf16[1,128,512]{2,1,0:T(8,128)(2,1)}, u32[]{:S(2)}, u32[]{:S(2)}) collective-permute-start(bf16[1,128,512]{2,1,0:T(8,128)(2,1)S(1)} %get-tuple-element.132), channel_id=1, source_target_pairs={{0,2},{1,3},{2,0},{3,1},{4,6},{5,7},{6,4},{7,5},{8,10},{9,11},{10,... | collective-permute-start | bytes 393224 | tf_op jit(solution)/shard_map/ppermute | solution.py:41
  70.9 29.7 %collective-permute-start.16 = (bf16[2,4,128,512]{3,2,1,0:T(8,128)(2,1)S(1)}, bf16[2,4,128,512]{3,2,1,0:T(8,128)(2,1)S(1)}, u32[]{:S(2)}, u32[]{:S(2)}) collective-permute-start(bf16[2,4,128,512]{3,2,1,0:T(8,128)(2,1)S(1)} %get-tuple-element.95), channel_id=1, source_target_pairs={{0,8},{4,12},{8,0},{12,4},{16,24},{20,28},{24,16},{28,20},{1,9},{5... | collective-permute-start | bytes 3145736 | tf_op jit(solution)/shard_map/ppermute | solution.py:36
  83.8 33.7 %collective-permute-start.10 = (bf16[2,4,128,512]{3,2,1,0:T(8,128)(2,1)S(1)}, bf16[2,4,128,512]{3,2,1,0:T(8,128)(2,1)S(1)}, u32[]{:S(2)}, u32[]{:S(2)}) collective-permute-start(bf16[2,4,128,512]{3,2,1,0:T(8,128)(2,1)S(1)} %get-tuple-element.97), channel_id=1, source_target_pairs={{0,16},{4,20},{8,24},{12,28},{16,0},{20,4},{24,8},{28,12},{1,17},{... | collective-permute-start | bytes 3145736 | tf_op jit(solution)/shard_map/ppermute | solution.py:36
  96.9 29.4 %collective-permute-start.27 = (bf16[128,2048]{1,0:T(8,128)(2,1)S(1)}, bf16[128,2048]{1,0:T(8,128)(2,1)S(1)}, u32[]{:S(2)}, u32[]{:S(2)}) collective-permute-start(bf16[128,2048]{1,0:T(8,128)(2,1)S(1)} %get-tuple-element.125), channel_id=1, source_target_pairs={{0,16},{4,20},{8,24},{12,28},{16,0},{20,4},{24,8},{28,12},{1,17},{... | collective-permute-start | bytes 1572872 | tf_op jit(solution)/shard_map/ppermute | solution.py:36
  99.0 29.1 %collective-permute-start.21 = (bf16[128,2048]{1,0:T(8,128)(2,1)S(1)}, bf16[128,2048]{1,0:T(8,128)(2,1)S(1)}, u32[]{:S(2)}, u32[]{:S(2)}) collective-permute-start(bf16[128,2048]{1,0:T(8,128)(2,1)S(1)} %get-tuple-element.127), channel_id=1, source_target_pairs={{0,8},{4,12},{8,0},{12,4},{16,24},{20,28},{24,16},{28,20},{1,9},{5... | collective-permute-start | bytes 1572872 | tf_op jit(solution)/shard_map/ppermute | solution.py:36
  100.7 43.4 %collective-permute-start.40 = (bf16[2,128,2048]{2,1,0:T(8,128)(2,1)}, bf16[2,128,2048]{2,1,0:T(8,128)(2,1)}, u32[]{:S(2)}, u32[]{:S(2)}) collective-permute-start(bf16[2,128,2048]{2,1,0:T(8,128)(2,1)} %get-tuple-element.87), channel_id=1, source_target_pairs={{0,8},{4,12},{8,0},{12,4},{16,24},{20,28},{24,16},{28,20},{1,9},{5... | collective-permute-start | bytes 3145736 | tf_op jit(solution)/shard_map/ppermute | solution.py:36
  117.5 56.1 %collective-permute-start.17 = (bf16[4,4,128,512]{3,2,1,0:T(8,128)(2,1)S(1)}, bf16[4,4,128,512]{3,2,1,0:T(8,128)(2,1)}, u32[]{:S(2)}, u32[]{:S(2)}) collective-permute-start(bf16[4,4,128,512]{3,2,1,0:T(8,128)(2,1)S(1)} %bitcast.369), channel_id=1, source_target_pairs={{0,4},{4,0},{8,12},{12,8},{16,20},{20,16},{24,28},{28,24},{1,5},{5... | collective-permute-start | bytes 6291464 | tf_op jit(solution)/shard_map/ppermute | solution.py:36
  118.9 55.1 %collective-permute-start.11 = (bf16[4,4,128,512]{3,2,1,0:T(8,128)(2,1)}, bf16[4,4,128,512]{3,2,1,0:T(8,128)(2,1)}, u32[]{:S(2)}, u32[]{:S(2)}) collective-permute-start(bf16[4,4,128,512]{3,2,1,0:T(8,128)(2,1)} %bitcast.13.own_a), channel_id=1, source_target_pairs={{0,4},{4,0},{8,12},{12,8},{16,20},{20,16},{24,28},{28,24},{1,5},{5... | collective-permute-start | bytes 6291464 | tf_op jit(solution)/shard_map/ppermute | solution.py:36
  128.9 31.0 %collective-permute-start.28 = (bf16[2,128,2048]{2,1,0:T(8,128)(2,1)}, bf16[2,128,2048]{2,1,0:T(8,128)(2,1)}, u32[]{:S(2)}, u32[]{:S(2)}) collective-permute-start(bf16[2,128,2048]{2,1,0:T(8,128)(2,1)} %get-tuple-element.91), channel_id=1, source_target_pairs={{0,8},{4,12},{8,0},{12,4},{16,24},{20,28},{24,16},{28,20},{1,9},{5... | collective-permute-start | bytes 3145736 | tf_op jit(solution)/shard_map/ppermute | solution.py:36
  152.7 69.3 %collective-permute-start.41 = (bf16[512,2048]{1,0:T(8,128)(2,1)}, bf16[512,2048]{1,0:T(8,128)(2,1)}, u32[]{:S(2)}, u32[]{:S(2)}) collective-permute-start(bf16[512,2048]{1,0:T(8,128)(2,1)} %bitcast.55.refs_4_.refs_3_), channel_id=1, source_target_pairs={{0,4},{4,0},{8,12},{12,8},{16,20},{20,16},{24,28},{28,24},{1,5},{5... | collective-permute-start | bytes 6291464 | tf_op jit(solution)/shard_map/ppermute | solution.py:36
  159.9 62.2 %collective-permute-start.35 = (bf16[512,2048]{1,0:T(8,128)(2,1)}, bf16[512,2048]{1,0:T(8,128)(2,1)}, u32[]{:S(2)}, u32[]{:S(2)}) collective-permute-start(bf16[512,2048]{1,0:T(8,128)(2,1)} %bitcast.49.refs_2_.refs_1_), channel_id=1, source_target_pairs={{0,4},{4,0},{8,12},{12,8},{16,20},{20,16},{24,28},{28,24},{1,5},{5... | collective-permute-start | bytes 6291464 | tf_op jit(solution)/shard_map/ppermute | solution.py:36
  171.9 71.7 %collective-permute-start.29 = (bf16[512,2048]{1,0:T(8,128)(2,1)}, bf16[512,2048]{1,0:T(8,128)(2,1)}, u32[]{:S(2)}, u32[]{:S(2)}) collective-permute-start(bf16[512,2048]{1,0:T(8,128)(2,1)} %bitcast.42.refs_4_.refs_3_), channel_id=1, source_target_pairs={{0,4},{4,0},{8,12},{12,8},{16,20},{20,16},{24,28},{28,24},{1,5},{5... | collective-permute-start | bytes 6291464 | tf_op jit(solution)/shard_map/ppermute | solution.py:36
  173.5 70.1 %collective-permute-start.23 = (bf16[512,2048]{1,0:T(8,128)(2,1)}, bf16[512,2048]{1,0:T(8,128)(2,1)}, u32[]{:S(2)}, u32[]{:S(2)}) collective-permute-start(bf16[512,2048]{1,0:T(8,128)(2,1)} %bitcast.36.refs_2_.refs_1_), channel_id=1, source_target_pairs={{0,4},{4,0},{8,12},{12,8},{16,20},{20,16},{24,28},{28,24},{1,5},{5... | collective-permute-start | bytes 6291464 | tf_op jit(solution)/shard_map/ppermute | solution.py:36
  372.0 50.3 %collective-permute-start.60 = (bf16[512,2048]{1,0:T(8,128)(2,1)}, bf16[512,2048]{1,0:T(8,128)(2,1)}, u32[]{:S(2)}, u32[]{:S(2)}) collective-permute-start(bf16[512,2048]{1,0:T(8,128)(2,1)} %convolution_convert_fusion.3), channel_id=1, source_target_pairs={{0,4},{4,0},{8,12},{12,8},{16,20},{20,16},{24,28},{28,24},{1,5},{5... | collective-permute-start | bytes 6291464 | tf_op jit(solution)/shard_map/ppermute | solution.py:36
  380.4 51.6 %collective-permute-start.72 = (bf16[512,2048]{1,0:T(8,128)(2,1)}, bf16[512,2048]{1,0:T(8,128)(2,1)}, u32[]{:S(2)}, u32[]{:S(2)}) collective-permute-start(bf16[512,2048]{1,0:T(8,128)(2,1)} %convolution_convert_fusion.1), channel_id=1, source_target_pairs={{0,4},{4,0},{8,12},{12,8},{16,20},{20,16},{24,28},{28,24},{1,5},{5... | collective-permute-start | bytes 6291464 | tf_op jit(solution)/shard_map/ppermute | solution.py:36
  422.3 41.7 %collective-permute-start.48 = (bf16[512,2048]{0,1:T(8,128)(2,1)}, bf16[512,2048]{0,1:T(8,128)(2,1)}, u32[]{:S(2)}, u32[]{:S(2)}) collective-permute-start(bf16[512,2048]{0,1:T(8,128)(2,1)} %pad_maximum_fusion.7), channel_id=1, source_target_pairs={{0,4},{4,0},{8,12},{12,8},{16,20},{20,16},{24,28},{28,24},{1,5},{5... | collective-permute-start | bytes 6291464 | tf_op jit(solution)/shard_map/ppermute | solution.py:36
  427.5 40.6 %collective-permute-start.61 = (bf16[2,128,2048]{1,2,0:T(8,128)(2,1)}, bf16[2,128,2048]{1,2,0:T(8,128)(2,1)}, u32[]{:S(2)}, u32[]{:S(2)}) collective-permute-start(bf16[2,128,2048]{1,2,0:T(8,128)(2,1)} %bitcast.121), channel_id=1, source_target_pairs={{0,8},{4,12},{8,0},{12,4},{16,24},{20,28},{24,16},{28,20},{1,9},{5... | collective-permute-start | bytes 3145736 | tf_op jit(solution)/shard_map/ppermute | solution.py:36
  459.7 45.0 %collective-permute-start.79 = (bf16[2,128,2048]{1,2,0:T(8,128)(2,1)}, bf16[2,128,2048]{1,2,0:T(8,128)(2,1)}, u32[]{:S(2)}, u32[]{:S(2)}) collective-permute-start(bf16[2,128,2048]{1,2,0:T(8,128)(2,1)} %copy.104), channel_id=1, source_target_pairs={{0,16},{4,20},{8,24},{12,28},{16,0},{20,4},{24,8},{28,12},{1,17},{... | collective-permute-start | bytes 3145736 | tf_op jit(solution)/shard_map/ppermute | solution.py:36
  464.0 63.0 %collective-permute-start.43 = (bf16[512,2,512]{0,2,1:T(8,128)(2,1)S(1)}, bf16[512,2,512]{0,2,1:T(8,128)(2,1)S(1)}, u32[]{:S(2)}, u32[]{:S(2)}) collective-permute-start(bf16[512,2,512]{0,2,1:T(8,128)(2,1)S(1)} %dynamic-slice_bitcast_fusion.1), channel_id=1, source_target_pairs={{0,16},{4,20},{8,24},{12,28},{16,0},{20,4},{24,8},{28,12},{1,17},{... | collective-permute-start | bytes 3145736 | tf_op jit(solution)/shard_map/ppermute | solution.py:36
  468.1 60.2 %collective-permute-start.49 = (bf16[512,2,512]{0,2,1:T(8,128)(2,1)S(1)}, bf16[512,2,512]{0,2,1:T(8,128)(2,1)S(1)}, u32[]{:S(2)}, u32[]{:S(2)}) collective-permute-start(bf16[512,2,512]{0,2,1:T(8,128)(2,1)S(1)} %dynamic-slice_bitcast_fusion), channel_id=1, source_target_pairs={{0,8},{4,12},{8,0},{12,4},{16,24},{20,28},{24,16},{28,20},{1,9},{5... | collective-permute-start | bytes 3145736 | tf_op jit(solution)/shard_map/ppermute | solution.py:36
  477.4 60.8 %collective-permute-start.62 = (bf16[128,2048]{0,1:T(8,128)(2,1)S(1)}, bf16[128,2048]{0,1:T(8,128)(2,1)S(1)}, u32[]{:S(2)}, u32[]{:S(2)}) collective-permute-start(bf16[128,2048]{0,1:T(8,128)(2,1)S(1)} %slice_bitcast_fusion.6), channel_id=1, source_target_pairs={{0,16},{4,20},{8,24},{12,28},{16,0},{20,4},{24,8},{28,12},{1,17},{... | collective-permute-start | bytes 1572872 | tf_op jit(solution)/shard_map/ppermute | solution.py:36
  482.2 67.3 %collective-permute-start.68 = (bf16[128,2048]{0,1:T(8,128)(2,1)S(1)}, bf16[128,2048]{0,1:T(8,128)(2,1)S(1)}, u32[]{:S(2)}, u32[]{:S(2)}) collective-permute-start(bf16[128,2048]{0,1:T(8,128)(2,1)S(1)} %slice_bitcast_fusion.4), channel_id=1, source_target_pairs={{0,16},{4,20},{8,24},{12,28},{16,0},{20,4},{24,8},{28,12},{1,17},{... | collective-permute-start | bytes 1572872 | tf_op jit(solution)/shard_map/ppermute | solution.py:36
  504.7 46.0 %collective-permute-start.74 = (bf16[128,2048]{0,1:T(8,128)(2,1)S(1)}, bf16[128,2048]{0,1:T(8,128)(2,1)S(1)}, u32[]{:S(2)}, u32[]{:S(2)}) collective-permute-start(bf16[128,2048]{0,1:T(8,128)(2,1)S(1)} %slice_bitcast_fusion.2), channel_id=1, source_target_pairs={{0,8},{4,12},{8,0},{12,4},{16,24},{20,28},{24,16},{28,20},{1,9},{5... | collective-permute-start | bytes 1572872 | tf_op jit(solution)/shard_map/ppermute | solution.py:36
  (114 other events, 1263.5 us)

commit v2 on v1

--- a/solution.py
+++ b/solution.py
@@ -9,7 +9,7 @@
 
 HEADS = 16
 HEAD = 64
-CHUNKS = 2
+SUBS = 4
 VMEM_LIMIT = 56 * 1024 * 1024
 
 f32 = jnp.float32
@@ -36,31 +36,35 @@
     return lax.ppermute(v, "wide", [(w, w ^ mask) for w in range(size)])
 
 
-def shift_narrow(v, step):
+def swap_narrow(v, mask):
     size = lax.axis_size("narrow")
-    return lax.ppermute(v, "narrow", [(z, (z + step) % size) for z in range(size)])
+    return lax.ppermute(v, "narrow", [(z, z ^ mask) for z in range(size)])
 
 
 def chip_bits():
     return (lax.axis_size("wide") // 2).bit_length() - 1
 
 
+def narrow_bits():
+    return lax.axis_size("narrow").bit_length() - 1
+
+
+def turned(index, bits):
+    out = 0
+    for bit in range(bits):
+        out = out + ((index >> bit) & 1) * (1 << (bits - 1 - bit))
+    return out
+
+
 def gather_narrow(v, axis):
-    size = lax.axis_size("narrow")
-    pieces = [v] + [shift_narrow(v, s) for s in range(1, size)]
-    return jnp.concatenate(pieces, axis)
-
-
-def gather_chips(v, order):
-    bits = chip_bits()
-    done = []
-    for bit in order:
-        other = swap_wide(v, 2 << bit)
-        axis = sum(1 for b in done if b > bit)
-        v = jnp.stack([v, other], axis)
-        done.append(bit)
-    assert len(done) == bits
+    for bit in reversed(range(narrow_bits())):
+        v = jnp.concatenate([v, swap_narrow(v, 1 << bit)], axis)
     return v
+
+
+def hop(v, done, bit):
+    axis = sum(1 for b in done if b > bit)
+    return jnp.stack([v, swap_wide(v, 2 << bit)], axis), done + [bit]
 
 
 def bit_of(index, bit):
@@ -99,8 +103,42 @@
     return t.reshape(v.shape)
 
 
+def slot_lanes(pos, block, wide, lanes):
+    at = ((block % 2) ^ pos[1]) * (wide // 2) + ((block // 2) ^ pos[0])
+    return pl.ds(pl.multiple_of(at * lanes, lanes), lanes)
+
+
+def whole_lanes(pos, slot, wide, lanes):
+    core, chip = divmod(slot, wide // 2)
+    at = (chip ^ pos[0]) * 2 + (core ^ pos[1])
+    return pl.ds(pl.multiple_of(at * lanes, lanes), lanes)
+
+
+def permute_kernel(wide, pos, v_ref, out_ref):
+    lanes = v_ref.shape[1] // wide
+    for b in range(wide):
+        out_ref[:, slot_lanes(pos, b, wide, lanes)] = v_ref[:, b * lanes : (b + 1) * lanes]
+
+
+def to_slots_quick(v, pos, chip, core):
+    wide = lax.axis_size("wide")
+    if (v.shape[1] // wide) % 128:
+        return to_slots(v, chip, core)
+    return pl.pallas_call(
+        functools.partial(permute_kernel, wide),
+        in_specs=[pl.BlockSpec(memory_space=pltpu.SMEM), pl.BlockSpec(memory_space=pltpu.VMEM)],
+        out_specs=pl.BlockSpec(memory_space=pltpu.VMEM),
+        out_shape=jax.ShapeDtypeStruct(v.shape, v.dtype),
+        name="permute",
+    )(pos, v)
+
+
+def after(v, *others):
+    return lax.optimization_barrier((v,) + others)[0]
+
+
 def load_rows(pos, geometry, own, other, matrix, first, count, place, sem):
-    narrow, per_matrix = geometry
+    narrow, per_matrix, rows = geometry[:3]
 
     def body(j, carry):
         block = matrix * per_matrix + first + j
@@ -108,15 +146,15 @@
         z = block % narrow
         chip = (w // 2) ^ pos[0]
         core = (w % 2) ^ pos[1]
-        step = lax.rem(pos[2] - z + narrow, narrow)
+        step = turned(z ^ pos[2], narrow.bit_length() - 1)
 
         @pl.when(core == 0)
         def _():
-            pltpu.make_async_copy(own.at[chip, step], place(j), sem).start()
+            pltpu.make_async_copy(own.at[chip, step, pl.ds(0, rows)], place(j), sem).start()
 
         @pl.when(core == 1)
         def _():
-            pltpu.make_async_copy(other.at[chip, step], place(j), sem).start()
+            pltpu.make_async_copy(other.at[chip, step, pl.ds(0, rows)], place(j), sem).start()
 
         return carry
 
@@ -129,9 +167,8 @@
 ):
     g = pl.program_id(0)
     steps = pl.num_programs(0)
-    rows = own_a.shape[2]
+    _, blocks, rows, wide = geometry
     sources = ((own_a, oth_a), (own_b, oth_b))
-    blocks = x_ref.shape[1] // rows
 
     @pl.when(g == 0)
     def _():
@@ -185,18 +222,22 @@
     def _():
         pltpu.make_async_copy(w_out, w_out, sems.at[2]).wait()
         width = w_out.shape[2]
+        lanes = 2 * width // wide
         for half in range(2):
             cols = slice(half * width, half * width + width)
-            h_ref[:, cols] = (
-                x_ref[:, cols].astype(f32) + dot(o_ref[...], w_out[half]) + bo_ref[0:1, cols]
-            )
+            hidden = x_ref[:, cols].astype(f32) + dot(o_ref[...], w_out[half]) + bo_ref[0:1, cols]
+            if lanes % 128:
+                h_ref[:, cols] = hidden
+            else:
+                for b in range(wide // 2):
+                    at = slot_lanes(pos, half * (wide // 2) + b, wide, lanes)
+                    h_ref[:, at] = hidden[:, b * lanes : (b + 1) * lanes]
 
 
 def run_attend_forward(pos, tokens, segment_ids, biases, own_a, oth_a, own_b, oth_b):
     count, features = tokens.shape
-    rows = own_a.shape[2]
-    narrow = own_a.shape[1]
-    geometry = (narrow, features // rows)
+    rows = own_b.shape[2]
+    geometry = (own_b.shape[1], features // rows, rows, own_b.shape[0] * 2)
     groups = features // 256
     whole = lambda *shape: pl.BlockSpec(shape, lambda g, pos: (0,) * len(shape))
     column = pl.BlockSpec((count, 256), lambda g, pos: (0, g))
@@ -246,14 +287,13 @@
 
 
 def attend_backward(
-    geometry, half, pos, dh_ref, add_ref, q_ref, k_ref, v_ref, p_ref, own_a, oth_a, own_b, oth_b,
-    d_ref, dx_ref, bias_ref, w_in, w_out, sems,
+    geometry, half, pos, dh_ref, add_ref, q_ref, k_ref, v_ref, p_ref, x_own, x_oth, o_own, o_oth,
+    own_a, oth_a, own_b, oth_b, gown_ref, goth_ref, dx_ref, bias_ref, w_in, w_out, sems,
 ):
     g = pl.program_id(0)
-    rows = own_a.shape[2]
     features = dh_ref.shape[1]
+    _, blocks, rows, _ = geometry
     sources = ((own_a, oth_a), (own_b, oth_b))
-    blocks = features // rows
 
     @pl.when(g == 0)
     def _():
@@ -308,7 +348,11 @@
             store.append(value.astype(bf16))
     joined = [jnp.concatenate(s, 1) for s in lows]
     for m in range(3):
-        d_ref[m] = joined[m]
+        goth_ref[m] = dot(x_oth[...], joined[m]).astype(bf16)
+        gown_ref[m] = dot(x_own[...], joined[m]).astype(bf16)
+    low = dh_ref[:, pl.ds(pl.multiple_of(half * width + g * 256, 256), 256)].astype(bf16)
+    goth_ref[3] = dot(o_oth[...], low).astype(bf16)
+    gown_ref[3] = dot(o_own[...], low).astype(bf16)
     bias_ref[...] = jnp.concatenate(
         [jnp.concatenate(s, 1) for s in sums] + [jnp.zeros((6, 256), f32)], 0
     )
@@ -325,11 +369,12 @@
     )
 
 
-def run_attend_backward(half, pos, grad_sum, added, q, k, v, probs, own_a, oth_a, own_b, oth_b):
+def run_attend_backward(half, pos, grad_sum, added, kept, rows_of, weights):
+    q, k, v, probs = kept
+    own_a, oth_a, own_b, oth_b = weights
     count, features = q.shape
-    rows = own_a.shape[2]
-    narrow = own_a.shape[1]
-    geometry = (narrow, features // rows)
+    rows = own_b.shape[2]
+    geometry = (own_b.shape[1], features // rows, rows, own_b.shape[0] * 2)
     groups = features // 512
     whole = lambda *shape: pl.BlockSpec(shape, lambda g, pos: (0,) * len(shape))
     column = pl.BlockSpec((count, 256), lambda g, pos: (0, half * groups + g))
@@ -343,10 +388,12 @@
             in_specs=[
                 whole(count, features), whole(count, features), column, column, column,
                 pl.BlockSpec((4, count, count), lambda g, pos: (half * groups + g, 0, 0)),
+                whole(width, count), whole(width, count), whole(width, count), whole(width, count),
                 anywhere, anywhere, anywhere, anywhere,
             ],
             out_specs=[
-                pl.BlockSpec((3, count, 256), lambda g, pos: (0, 0, g)),
+                pl.BlockSpec((4, width, 256), lambda g, pos: (0, 0, g)),
+                pl.BlockSpec((4, width, 256), lambda g, pos: (0, 0, g)),
                 whole(count, features),
                 pl.BlockSpec((8, 256), lambda g, pos: (0, g)),
             ],
@@ -357,7 +404,8 @@
             ],
         ),
         out_shape=[
-            jax.ShapeDtypeStruct((3, count, width), bf16),
+            jax.ShapeDtypeStruct((4, width, width), bf16),
+            jax.ShapeDtypeStruct((4, width, width), bf16),
             jax.ShapeDtypeStruct((count, features), f32),
             jax.ShapeDtypeStruct((8, width), f32),
         ],
@@ -368,7 +416,7 @@
             flops=2 * count * features * features * 6, bytes_accessed=16 << 20, transcendentals=0
         ),
         name="attend_backward",
-    )(pos, grad_sum, added, q, k, v, probs, own_a, oth_a, own_b, oth_b)
+    )(pos, grad_sum, added, q, k, v, probs, *rows_of, own_a, oth_a, own_b, oth_b)
 
 
 def moments(hidden):
@@ -403,8 +451,8 @@
     return [slice(r, r + ROWS_AT_ONCE) for r in range(0, count, ROWS_AT_ONCE)]
 
 
-def ffn_forward(first, last, *refs):
-    refs = list(refs)
+def ffn_forward(first, last, wide, *refs):
+    pos, *refs = refs
     h_ref, vec, w1a, w1b, w2a, w2b, b1 = refs[:7]
     refs = refs[7:]
     f_in = None if first else refs.pop(0)
@@ -413,8 +461,8 @@
     refs = refs[2:]
     u_out = refs.pop(0) if first else None
     if last:
-        result, dh, dh_low, sums = refs[:4]
-        refs = refs[4:]
+        result, dh, dh_low, dh_turned, sums = refs[:5]
+        refs = refs[5:]
         total, u_low = refs
     else:
         total, u_low = refs
@@ -428,7 +476,8 @@
             center, factor = moments(h_ref[r, :])
             u_low[r, :] = (center * factor * (1.0 + vec[0:1, :]) + vec[1:2, :]).astype(bf16)
         if first:
-            u_out[...] = u_low[...]
+            for r in row_blocks(count):
+                u_out[:, r] = u_low[r, :].T
             total[...] = jnp.zeros_like(total)
         else:
             total[...] = f_in[...]
@@ -450,11 +499,21 @@
                 u = center * factor * (1.0 + vec[0:1, :]) + vec[1:2, :]
                 center, factor = moments(u + total[r, :] + vec[2:3, :])
                 normed = center * factor
-                result[r, :] = (normed * (1.0 + vec[3:4, :]) + vec[4:5, :]).astype(bf16)
+                final = (normed * (1.0 + vec[3:4, :]) + vec[4:5, :]).astype(bf16)
+                lanes = features // wide
+                if lanes % 128:
+                    result[r, :] = final
+                else:
+                    for slot in range(wide):
+                        result[r, whole_lanes(pos, slot, wide, lanes)] = final[
+                            :, slot * lanes : (slot + 1) * lanes
+                        ]
                 grad = dy[r, :].astype(f32)
                 back = norm_back(grad * (1.0 + vec[3:4, :]), normed, factor)
                 dh[r, :] = back
-                dh_low[r, :] = back.astype(bf16)
+                low = back.astype(bf16)
+                dh_low[r, :] = low
+                dh_turned[:, r] = low.T
                 sums[0:1, :] += jnp.sum(grad, 0, keepdims=True)
                 sums[1:2, :] += jnp.sum(grad * normed, 0, keepdims=True)
                 sums[2:3, :] += jnp.sum(back, 0, keepdims=True)
@@ -463,15 +522,16 @@
 TILE = 512
 
 
-def run_ffn_forward(hidden, vec, w1, w2, b1, earlier, dy):
+def run_ffn_forward(pos, hidden, vec, w1, w2, b1, earlier, dy):
     count, features = hidden.shape
     width, units = w1[0].shape
     first, last = earlier is None, dy is not None
     whole = lambda *shape: pl.BlockSpec(shape, lambda t: (0,) * len(shape))
     tall = pl.BlockSpec((width, TILE), lambda t: (0, t))
     strip = pl.BlockSpec((count, TILE), lambda t: (0, t))
-    ins = [hidden, vec, w1[0], w1[1], w2[0], w2[1], b1]
+    ins = [pos, hidden, vec, w1[0], w1[1], w2[0], w2[1], b1]
     in_specs = [
+        pl.BlockSpec(memory_space=pltpu.SMEM),
         whole(count, features), whole(8, features), tall, tall, tall, tall,
         pl.BlockSpec((1, TILE), lambda t: (0, t)),
     ]
@@ -485,14 +545,15 @@
         ins.append(dy)
         in_specs.append(whole(count, features))
     if first:
-        out_specs.append(whole(count, features))
-        out_shape.append(jax.ShapeDtypeStruct((count, features), bf16))
+        out_specs.append(whole(features, count))
+        out_shape.append(jax.ShapeDtypeStruct((features, count), bf16))
     if last:
-        out_specs += [whole(count, features)] * 3 + [whole(8, features)]
+        out_specs += [whole(count, features)] * 3 + [whole(features, count), whole(8, features)]
         out_shape += [
             jax.ShapeDtypeStruct((count, features), bf16),
             jax.ShapeDtypeStruct((count, features), f32),
             jax.ShapeDtypeStruct((count, features), bf16),
+            jax.ShapeDtypeStruct((features, count), bf16),
             jax.ShapeDtypeStruct((8, features), f32),
         ]
         scratch = [pltpu.VMEM((count, features), f32)] + scratch
@@ -500,7 +561,7 @@
         out_specs.append(whole(count, features))
         out_shape.append(jax.ShapeDtypeStruct((count, features), f32))
     return pl.pallas_call(
-        functools.partial(ffn_forward, first, last),
+        functools.partial(ffn_forward, first, last, lax.axis_size("wide")),
         grid=(units // TILE,),
         in_specs=in_specs,
         out_specs=out_specs,
@@ -516,16 +577,14 @@
     )(*ins)
 
 
-def ffn_backward(first, last, *refs):
-    refs = list(refs)
-    dh_low, w1a, w1b, w2a, w2b, slope = refs[:6]
-    refs = refs[6:]
+def ffn_backward(first, last, wide, *refs):
+    pos, dh_low, dh_turned, u_turned, w1a, w1b, w2a, w2b, act, slope, *refs = refs
     du_in = None if first else refs.pop(0)
     if last:
         dh, h_ref, vec = refs[:3]
         refs = refs[3:]
-    da_ref, db_ref = refs[:2]
-    refs = refs[2:]
+    own_ref, oth_ref, db_ref = refs[:3]
+    refs = refs[3:]
     if last:
         dh1, sums, total = refs
     else:
@@ -538,11 +597,22 @@
     def _():
         total[...] = jnp.zeros_like(total) if first else du_in[...]
 
+    active = act[...]
+    block = features // wide
+
+    def store(ref, which, value):
+        value = value.astype(bf16)
+        for k in range(wide // 2):
+            ref[k, which] = value[k * block : (k + 1) * block]
+
+    store(oth_ref, 1, dot(dh_turned[width:, :], active))
+    store(own_ref, 1, dot(dh_turned[:width, :], active))
     grad = dot(dh_low[:, :width], w2a[...]) + dot(dh_low[:, width:], w2b[...])
     grad = grad * slope[...].astype(f32)
     db_ref[...] = jnp.sum(grad, 0, keepdims=True)
     low = grad.astype(bf16)
-    da_ref[...] = low
+    store(oth_ref, 0, dot(u_turned[width:, :], low))
+    store(own_ref, 0, dot(u_turned[:width, :], low))
     total[:, :width] += dot_nt(low, w1a[...])
     total[:, width:] += dot_nt(low, w1b[...])
     if last:
@@ -550,29 +620,45 @@
         @pl.when(t == pl.num_programs(0) - 1)
         def _():
             sums[...] = jnp.zeros_like(sums)
+            lanes = features // wide
             for r in row_blocks(count):
                 center, factor = moments(h_ref[r, :])
                 normed = center * factor
                 du = total[r, :] + dh[r, :]
                 back = norm_back(du * (1.0 + vec[0:1, :]), normed, factor)
-                dh1[r, :] = back
+                if lanes % 128:
+                    dh1[r, :] = back
+                else:
+                    for slot in range(wide):
+                        dh1[r, whole_lanes(pos, slot, wide, lanes)] = back[
+                            :, slot * lanes : (slot + 1) * lanes
+                        ]
                 sums[0:1, :] += jnp.sum(du, 0, keepdims=True)
                 sums[1:2, :] += jnp.sum(du * normed, 0, keepdims=True)
                 sums[2:3, :] += jnp.sum(back, 0, keepdims=True)
 
 
-def run_ffn_backward(dh_low, w1, w2, slope, earlier, tail):
+def run_ffn_backward(sub, units, pos, dh_low, dh_turned, u_turned, w1, w2, act, slope, earlier, tail):
     count, features = dh_low.shape
-    width, units = w1[0].shape
+    width = w1[0].shape[0]
+    wide = lax.axis_size("wide")
     first, last = earlier is None, tail is not None
+    tiles = units // TILE
     whole = lambda *shape: pl.BlockSpec(shape, lambda t: (0,) * len(shape))
-    tall = pl.BlockSpec((width, TILE), lambda t: (0, t))
-    strip = pl.BlockSpec((count, TILE), lambda t: (0, t))
-    ins = [dh_low, w1[0], w1[1], w2[0], w2[1], slope]
-    in_specs = [whole(count, features), tall, tall, tall, tall, strip]
-    out_specs = [strip, pl.BlockSpec((1, TILE), lambda t: (0, t))]
+    tall = pl.BlockSpec((width, TILE), lambda t: (0, sub * tiles + t))
+    strip = pl.BlockSpec((count, TILE), lambda t: (0, sub * tiles + t))
+    ins = [pos, dh_low, dh_turned, u_turned, w1[0], w1[1], w2[0], w2[1], act, slope]
+    in_specs = [
+        pl.BlockSpec(memory_space=pltpu.SMEM),
+        whole(count, features), whole(features, count), whole(features, count),
+        tall, tall, tall, tall, strip, strip,
+    ]
+    shape = (wide // 2, 2, features // wide, units)
+    grads = pl.BlockSpec(shape[:3] + (TILE,), lambda t: (0, 0, 0, t))
+    out_specs = [grads, grads, pl.BlockSpec((1, TILE), lambda t: (0, t))]
     out_shape = [
-        jax.ShapeDtypeStruct((count, units), bf16),
+        jax.ShapeDtypeStruct(shape, bf16),
+        jax.ShapeDtypeStruct(shape, bf16),
         jax.ShapeDtypeStruct((1, units), f32),
     ]
     scratch = []
@@ -592,8 +678,8 @@
         out_specs.append(whole(count, features))
         out_shape.append(jax.ShapeDtypeStruct((count, features), f32))
     return pl.pallas_call(
-        functools.partial(ffn_backward, first, last),
-        grid=(units // TILE,),
+        functools.partial(ffn_backward, first, last, lax.axis_size("wide")),
+        grid=(tiles,),
         in_specs=in_specs,
         out_specs=out_specs,
         out_shape=out_shape,
@@ -602,56 +688,76 @@
             vmem_limit_bytes=VMEM_LIMIT, dimension_semantics=("arbitrary",)
         ),
         cost_estimate=pl.CostEstimate(
-            flops=4 * count * features * units * 2, bytes_accessed=16 << 20, transcendentals=0
+            flops=8 * count * features * units, bytes_accessed=16 << 20, transcendentals=0
         ),
         name="ffn_backward",
     )(*ins)
 
 
-def add_low(a, b):
-    return (a.astype(f32) + b.astype(f32)).astype(bf16)
-
-
-def scatter_ffn(own, other, order):
-    bits = chip_bits()
-    narrow = lax.axis_size("narrow")
-    received = swap_wide(other().astype(bf16), 1)
-    part = (own() + received.astype(f32)).astype(bf16)
-    rows, columns = part.shape
-    part = part.reshape((2,) * bits + (rows >> bits, columns))
-    left = list(range(bits - 1, -1, -1))
-    for bit in order:
-        axis = left.index(bit)
-        received = swap_wide(lax.index_in_dim(part, 1, axis, keepdims=False), 2 << bit)
-        part = add_low(lax.index_in_dim(part, 0, axis, keepdims=False), received)
-        left.remove(bit)
-    part = part.reshape(rows >> bits, narrow, columns // narrow)
-    total = part[:, 0].astype(f32)
-    for s in range(1, narrow):
-        total = total + shift_narrow(part[:, narrow - s], s).astype(f32)
-    return total
-
-
-def scatter_attn(own, other, order, chip, z, rows_each):
-    bits = chip_bits()
-    narrow = lax.axis_size("narrow")
-    received = swap_wide(other().astype(bf16), 1)
-    part = (own() + received.astype(f32)).astype(bf16)
-    low_bits = bits - 2
-    columns = part.shape[1] // 4
-    part = part.reshape((2,) * low_bits + (narrow * rows_each, 2, 2, columns))
-    names = list(range(low_bits - 1, -1, -1)) + [None, bits - 1, bits - 2, None]
-    for bit in order:
-        axis = names.index(bit)
-        mine = bit_of(chip, bit)
-        received = swap_wide(pick(part, axis, 1 - mine), 2 << bit)
-        part = add_low(pick(part, axis, mine), received)
-        names.pop(axis)
-    part = part.reshape(narrow, rows_each, columns)
-    total = pick(part, 0, z).astype(f32)
-    for s in range(1, narrow):
-        total = total + shift_narrow(pick(part, 0, lax.rem(z + s, narrow)), s).astype(f32)
-    return total
+def swap_hop(v, hop):
+    kind, bit = hop
+    return swap_wide(v, 2 << bit) if kind == "wide" else swap_narrow(v, 1 << bit)
+
+
+class Scatter:
+    def __init__(self, own, other, axes, mine, extra=None):
+        self.parts = [(own, ())]
+        self.other = other
+        self.axes, self.mine = dict(axes), mine
+        self.extra = [] if extra is None else [(extra[0], ())]
+        self.extra_other = None if extra is None else extra[1]
+
+    def cross(self):
+        own = self.parts[0][0]
+        self.parts.append((swap_wide(self.other, 1).reshape(own.shape), ()))
+        if self.extra:
+            self.extra.append((swap_wide(self.extra_other, 1), ()))
+
+    def send(self, hop):
+        self.hop = hop
+        axis = self.axes.pop(hop, None)
+        keep = 0 if axis is None else self.mine[hop]
+        more = lambda parts, i: [(v, path + ((axis, i),)) for v, path in parts]
+        self.leaving = low_of(more(self.parts, 1 - keep))
+        self.parts = more(self.parts, keep)
+        if self.extra:
+            self.leaving = jnp.concatenate([self.leaving, low_of(more(self.extra, 1 - keep))], -2)
+            self.extra = more(self.extra, keep)
+        if axis is not None:
+            self.axes = {h: a - (a > axis) for h, a in self.axes.items()}
+        return self.leaving
+
+    def receive(self):
+        came = swap_hop(self.leaving, self.hop)
+        if self.extra:
+            rows = self.parts[0][0].shape[-2]
+            self.extra.append((came[..., rows:, :], ()))
+            came = came[..., :rows, :]
+        self.parts.append((came, ()))
+
+    def hold(self, *others):
+        self.parts = [(after(v, *others), path) for v, path in self.parts]
+
+
+def taken(part):
+    v, path = part
+    for axis, i in path:
+        if axis is None:
+            size = v.shape[-1] // 2
+            v = v[..., i * size : i * size + size]
+        elif isinstance(i, int):
+            v = lax.index_in_dim(v, i, axis, keepdims=False)
+        else:
+            v = pick(v, axis, i)
+    return v
+
+
+def sum_of(parts, view=lambda v: v):
+    return sum(view(taken(p)).astype(f32) for p in parts)
+
+
+def low_of(parts, view=lambda v: v):
+    return sum_of(parts, view).astype(bf16)
 
 
 def per_device(tokens, segment_ids, attn_weight, vectors, ffn_weight, ffn_bias, out_grad):
@@ -665,153 +771,193 @@
     count, features = tokens.shape
     half = features // 2
 
+    rows_each = attn_weight.shape[0]
     each, each_bias = vectors.shape[0], ffn_bias.shape[0]
-    room = -(-(each + each_bias) // 128) * 128
-    small = jnp.concatenate(
-        [vectors, ffn_bias, jnp.zeros((room - each - each_bias,), bf16)]
-    ).reshape(1, room)
-    small = gather_narrow(small, 0)
-    small = gather_chips(small, up).reshape(-1, room)
-    small = jnp.concatenate([small, swap_wide(small, 1)], 0)
+    small = jnp.concatenate([vectors, ffn_bias, jnp.zeros((features - each - each_bias,), bf16)])
+    small = jnp.concatenate([small[None], jnp.zeros((7, features), bf16)])
+    v = jnp.concatenate([attn_weight, small])
+    attn_whole = gather_narrow(v[None], 0)
+    units = ffn_weight.shape[2]
+    width = units // SUBS
+    tail = units - width
+    orders = (up, down)
+
+    def climb(trees, first, last, waits=()):
+        for step in range(first, last):
+            trees = [
+                (*hop(after(v, *waits) if waits else v, done, order[step]), order)
+                for v, done, order in trees
+            ]
+            waits = ()
+        return trees
+
+    late = climb([(ffn_weight[i, :, tail:], [], orders[i]) for i in range(2)], 0, bits)
+    attn = [
+        (attn_whole[:, :, :half], [], up),
+        (attn_whole[:, :rows_each, half:], [], down),
+    ]
+    attn = climb(attn, 0, 1, [v for v, _, _ in late])
+    early_whole = gather_narrow(after(ffn_weight[:, :, :tail], attn_whole), 2)
+    v = jnp.stack([v.reshape(half, width) for v, _, _ in late])
+    late_whole = gather_narrow(after(v, early_whole), 2)
+    attn = climb(attn, 1, bits)
+    halves = []
+    for v, _, _ in attn:
+        v = v.reshape((wide // 2,) + v.shape[bits:])
+        halves += [v, swap_wide(v, 1)]
+    early = [
+        (
+            jnp.concatenate(
+                [
+                    early_whole[which, :, at * tail + sub * width :][:, :width]
+                    for sub in range(SUBS - 1)
+                    for at in range(narrow)
+                ],
+                1,
+            ),
+            [],
+            orders[which],
+        )
+        for which in range(2)
+    ]
+    early = climb(early, 0, 1, [halves[1], halves[3]])
+    tokens_now = after(tokens, late_whole)
+    early = climb(early, 1, bits)
+    late = [(late_whole[which], swap_wide(late_whole[which], 1)) for which in range(2)]
+
+    small = jnp.concatenate([h[:, :, rows_each, : each + each_bias] for h in halves[:2]])
+    small = small.reshape(-1, each + each_bias)
     slots = jnp.arange(wide * narrow)
     slot_core, slot_chip, slot_z = (
         slots // (wide * narrow // 2), (slots // narrow) % (wide // 2), slots % narrow,
     )
     slot_w = (slot_chip ^ chip) * 2 + (slot_core ^ core)
-    whole_at = slot_w * narrow + lax.rem(z - slot_z + narrow, narrow)
+    whole_at = slot_w * narrow + (turned(slot_z, narrow_bits()) ^ z)
     bias_at = slot_z * wide + slot_w
     spots = jnp.arange(wide * narrow)[:, None]
     vec_rows = dot((spots == whole_at[None, :]).astype(bf16), small[:, :each]).reshape(8, features)
-    bias_rel = dot(
-        (spots == bias_at[None, :]).astype(bf16), small[:, each : each + each_bias]
-    ).reshape(narrow, CHUNKS, -1)
+    bias_rel = dot((spots == bias_at[None, :]).astype(bf16), small[:, each:])
+    bias_rel = bias_rel.reshape(narrow, SUBS, width).transpose(1, 0, 2).reshape(SUBS, -1)
     bq, bv, bo, s1, bf, s2, g1, g2 = [vec_rows[i] for i in range(8)]
-    slot_vec = to_slots(jnp.stack([g1, s1, bf, g2, s2, s2, s2, s2]), chip, core)
-    dy = to_slots(out_grad, chip, core)
-
-    rows_each = attn_weight.shape[0]
-    halves = []
-    for part, order in ((0, up), (1, down)):
-        v = attn_weight[:, part * half : part * half + half].reshape(1, rows_each, half)
-        v = gather_narrow(v, 0)
-        v = gather_chips(v, order).reshape(wide // 2, narrow, rows_each, half)
-        halves += [v, swap_wide(v, 1)]
-
-    units = ffn_weight.shape[2] // CHUNKS
-    ffn = []
-    for c in range(CHUNKS):
-        pair = []
-        for which, order in ((0, up), (1, down)):
-            v = ffn_weight[which, :, c * units : c * units + units]
-            v = gather_narrow(v, 1)
-            v = gather_chips(v, order).reshape(-1, narrow * units)
-            pair.append((v, swap_wide(v, 1)))
-        ffn.append(pair)
+    slot_vec = to_slots_quick(jnp.stack([g1, s1, bf, g2, s2, s2, s2, s2]), pos, chip, core)
+    dy = to_slots_quick(out_grad, pos, chip, core)
+    in_kernel = (features // wide) % 128 == 0
+
+    def core_rows(v, which):
+        t = v.reshape(count, -1, 2, narrow * rows_each)
+        return pick(t, 2, which).reshape(count, half).T
+
+    x_rows = [core_rows(tokens, core), core_rows(tokens, 1 - core)]
 
     biases = jnp.stack([bq, bv, bo, bo, bo, bo, bo, bo])
-    q, k, v, probs, mixed, hidden = run_attend_forward(pos, tokens, segment_ids, biases, *halves)
-    hidden = to_slots(hidden, chip, core)
-    acts, slopes = [], []
+    *kept, mixed, hidden = run_attend_forward(pos, tokens_now, segment_ids, biases, *halves)
+    o_rows = [core_rows(mixed, core), core_rows(mixed, 1 - core)]
+    hidden = after(hidden, *o_rows)
+    if not in_kernel:
+        hidden = to_slots(hidden, chip, core)
+    early = [after(v.reshape(half, -1), hidden) for v, _, _ in early]
+    early = [(v, swap_wide(v, 1)) for v in early]
+    act_late, slope_late, u_turned, total = run_ffn_forward(
+        pos, hidden, slot_vec, *late, bias_rel[-1].reshape(1, -1), None, None
+    )
+    act, slope, result, dh, dh_low, dh_turned, sums_two = run_ffn_forward(
+        pos, hidden, slot_vec, *early, bias_rel[:-1].reshape(1, -1), total, dy
+    )
+    if not in_kernel:
+        result = from_slots(result, chip, core)
+
+    sources = [(0, late, act_late, slope_late)]
+    sources += [(sub, early, act, slope) for sub in range(SUBS - 1)]
     total = None
-    for c in range(CHUNKS):
-        b1 = bias_rel[:, c].reshape(1, -1)
-        outs = run_ffn_forward(
-            hidden, slot_vec, *ffn[c], b1, total, dy if c == CHUNKS - 1 else None
+    dbs, units = [], []
+    chips = lambda order: [("wide", bit) for bit in order]
+    along = [("narrow", bit) for bit in range(narrow_bits())]
+    routes = [along + chips(down), chips(down), chips(up), chips(down)]
+    low = dh_low
+    for j, (sub, weights, active, steep) in enumerate(sources):
+        outs = run_ffn_backward(
+            sub, narrow * width, pos, low, dh_turned, u_turned, *weights, active, steep, total,
+            (dh, hidden, slot_vec) if j == SUBS - 1 else None,
         )
-        acts.append(outs[0])
-        slopes.append(outs[1])
-        rest = outs[2:]
-        if c == 0:
-            u_low = rest[0]
-            rest = rest[1:]
-        if c < CHUNKS - 1:
-            total = rest[0]
-    result, dh, dh_low, sums_two = rest
-    result = from_slots(result, chip, core)
-
-    grad_down = [
-        scatter_ffn(
-            functools.partial(dot_tn, dh_low[:, :half], acts[c]),
-            functools.partial(dot_tn, dh_low[:, half:], acts[c]),
-            down,
-        )
-        for c in range(CHUNKS)
-    ]
-    total = None
-    das, dbs = [], []
-    for c in range(CHUNKS):
-        outs = run_ffn_backward(
-            dh_low, *ffn[c], slopes[c], total, (dh, hidden, slot_vec) if c == CHUNKS - 1 else None
-        )
-        das.append(outs[0])
-        dbs.append(outs[1])
-        total = outs[2]
-    grad_sum, sums_one = total, outs[3]
-    grad_up = [
-        scatter_ffn(
-            functools.partial(dot_tn, u_low[:, :half], das[c]),
-            functools.partial(dot_tn, u_low[:, half:], das[c]),
-            up,
-        )
-        for c in range(CHUNKS)
-    ]
-    grad_ffn = jnp.stack(
-        [jnp.concatenate(grad_up, -1), jnp.concatenate(grad_down, -1)]
-    )
-
-    grad_sum = from_slots(grad_sum, chip, core)
-    grad_low = grad_sum.astype(bf16)
-
-    def core_columns(v, which):
-        t = v.reshape(count, -1, 2, narrow * rows_each)
-        return pick(t, 2, which).reshape(count, half)
-
-    x_own, x_oth = core_columns(tokens, core), core_columns(tokens, 1 - core)
-    o_own, o_oth = core_columns(mixed, core), core_columns(mixed, 1 - core)
-    grad_tokens = grad_sum
-    grad_attn, bias_sums = [], []
-    for part, order in ((0, down), (1, up)):
-        grads, grad_tokens, bias_sum = run_attend_backward(
-            part, pos, grad_sum, grad_tokens, q, k, v, probs, *halves
+        shape = (2,) * bits + outs[0].shape[1:]
+        axes = {("wide", bit): bits - 1 - bit for bit in range(bits)}
+        unit = Scatter(outs[0].reshape(shape), outs[1], axes, dict.fromkeys(axes, 0))
+        unit.cross()
+        units.append(unit)
+        dbs.append(outs[2])
+        total = outs[3]
+        if j >= 1 and j < 3:
+            low = after(low, units[j - 1].send(routes[j - 1][0]))
+            units[j - 1].receive()
+    grad_sum, sums_one = total, outs[4]
+    if not in_kernel:
+        grad_sum = from_slots(grad_sum, chip, core)
+
+    low_bits = bits - 2
+    names = chips([bits - 1, bits - 2] + list(range(low_bits))[::-1]) + along[::-1]
+    attn_axes = {name: axis for axis, name in enumerate(names)}
+    mine = {("wide", bit): bit_of(chip, bit) for bit in range(bits)}
+    mine.update({("narrow", bit): bit_of(z, bit) for bit in range(narrow_bits())})
+    added = grad_sum
+    bias_sums, attn_units = [], []
+    slot_sums = from_slots(jnp.concatenate([sums_one[:3], sums_two[:3]]), chip, core)
+    gs1, gg1, gbo, gs2, gg2, gbf = [slot_sums[i] for i in range(6)]
+    dbs = dbs[1:] + dbs[:1]
+    db = jnp.stack([d.reshape(narrow, -1) for d in dbs], 1).reshape(narrow, wide, each_bias)
+    at = turned(jnp.arange(narrow) ^ z, narrow_bits())
+    db = jnp.stack([pick(db, 0, at[i]) for i in range(narrow)], 1)
+
+    def small_rows():
+        gbq = jnp.concatenate([bias_sums[0][0], bias_sums[1][0]])
+        gbv = jnp.concatenate([bias_sums[0][1], bias_sums[1][1]])
+        vec = jnp.concatenate([gbq, gbv, gbo, gs1, gbf, gs2, gg1, gg2]).reshape(wide, narrow, each)
+        rows = jnp.concatenate([vec, db], 2)
+        rows = jnp.pad(rows[:, :, None], ((0, 0), (0, 0), (0, 7), (0, half - each - each_bias)))
+        rows = rows.astype(bf16).reshape((2,) * (bits + 1 + narrow_bits()) + rows.shape[2:])
+        return pick(rows, bits, core), pick(rows, bits, 1 - core)
+
+    waiting = [[(2, 0), (3, 0), (1, 1), (0, 1)], [(2, 1), (3, 1), (0, 2)]]
+    for part in range(2):
+        leaving = []
+        for j, step in waiting[part]:
+            leaving.append(units[j].send(routes[j][step]))
+            units[j].receive()
+        low = after(grad_sum, *leaving)
+        own, other, added, bias_sum = run_attend_backward(
+            part, pos, low, added, kept, x_rows + o_rows, halves
         )
         bias_sums.append(bias_sum)
-        columns = slice(part * half, part * half + half)
-
-        def weights(x_rows, o_rows, grads=grads, columns=columns):
-            return jnp.concatenate(
-                [dot_tn(x_rows, grads[m]) for m in range(3)]
-                + [dot_tn(o_rows, grad_low[:, columns])],
-                1,
-            )
-
-        grad_attn.append(
-            scatter_attn(
-                functools.partial(weights, x_own, o_own),
-                functools.partial(weights, x_oth, o_oth),
-                order, chip, z, rows_each,
-            )
+        shape = (2,) * len(names) + (rows_each, half)
+        unit = Scatter(
+            own.reshape(shape), other, attn_axes, mine, None if part == 0 else small_rows()
         )
-    grad_attn = jnp.concatenate(grad_attn, 1)
-
-    slot_sums = from_slots(jnp.concatenate([sums_one[:3], sums_two[:3]]), chip, core)
-    gs1, gg1, gbo, gs2, gg2, gbf = [slot_sums[i] for i in range(6)]
-    gbq = jnp.concatenate([bias_sums[0][0], bias_sums[1][0]])
-    gbv = jnp.concatenate([bias_sums[0][1], bias_sums[1][1]])
-    vec = jnp.concatenate([gbq, gbv, gbo, gs1, gbf, gs2, gg1, gg2]).reshape(wide, narrow, each)
-    db = jnp.stack([d.reshape(narrow, -1) for d in dbs], 1).reshape(narrow, wide, each_bias)
-    part = jnp.concatenate([vec, db.transpose(1, 0, 2)], 2)
-    part = part.reshape((2,) * (bits + 1) + part.shape[1:])
-    for bit in range(bits + 1):
-        axis = bits - bit
-        mine = bit_of(w, bit)
-        part = pick(part, axis, mine) + swap_wide(pick(part, axis, 1 - mine), 1 << bit)
-    at = lambda s: jnp.concatenate(
-        [pick(part[:, :each], 0, lax.rem(z + s, narrow)), part[(narrow - s) % narrow, each:]]
+        unit.cross()
+        attn_units.append(unit)
+    grad_tokens = added
+
+    for unit in units:
+        unit.hold(added)
+    for unit, route in zip(units, routes):
+        for hop_to in route[3 if unit is units[0] else 2 :]:
+            unit.send(hop_to)
+            unit.receive()
+    rest = units[1:]
+    for hop_to in along:
+        leaving = [u.send(hop_to) for u in rest]
+        came = swap_hop(jnp.concatenate(leaving, -1), hop_to)
+        size = leaving[0].shape[-1]
+        for i, u in enumerate(rest):
+            u.parts.append((came[..., i * size : i * size + size], ()))
+    grad_ffn = jnp.concatenate([sum_of(u.parts) for u in rest + units[:1]], -1)
+    for step in range(bits + len(along)):
+        for unit, order in zip(attn_units, (down, up)):
+            unit.send((chips(order) + along)[step])
+            unit.receive()
+    grad_attn = jnp.concatenate([sum_of(u.parts) for u in attn_units], -1)
+    tally = sum_of(attn_units[1].extra)[0]
+    return (
+        result, grad_tokens, grad_attn, tally[:each], grad_ffn, tally[each : each + each_bias],
     )
-    tally = at(0)
-    for s in range(1, narrow):
-        tally = tally + shift_narrow(at(s), s)
-    return (result, grad_tokens, grad_attn, tally[:each], grad_ffn, tally[each:])
 
 
 def solution(mesh):

time: 628 us -> 479 us (0.76)
  starting transfers between devices: 123 us -> 50.2 us
  local copies, waits for them, and re-layouts: 105 us -> 51.7 us
  matrix products: 51.4 us -> 0.24 us
  Pallas kernels: 117 us -> 142 us
  other arithmetic: 68.1 us -> 50.1 us
  waiting for transfers between devices: 152 us -> 168 us
  between operations: 2.51 us -> 9.68 us
    ppermute x42 -> x14, waiting for transfers between devices: 31.5 us -> 106 us  [swap_narrow(): return lax.ppermute(v, 'narrow', [(z, z ^ mask) for z in range(size)])]
    ppermute x42 -> x14, starting transfers between devices: 84.7 us -> 17.4 us  [swap_narrow(): return lax.ppermute(v, 'narrow', [(z, z ^ mask) for z in range(size)])]
    ppermute x42 -> x37, waiting for transfers between devices: 120 us -> 62.6 us  [swap_wide(): return lax.ppermute(v, 'wide', [(w, w ^ mask) for w in range(size)])]
    dot_general x24 -> x0, matrix products: 50.4 us -> none  [dot_tn(): return lax.dot_general(a, b, TN, preferred_element_type=f32)]
    pallas_call x4 -> x8, Pallas kernels: 61.9 us -> 81.3 us  [the longest x4 45.4 us: run_ffn_backward(): pl.pallas_call(functools.partial(ffn_backward, first, last, lax.axis_size...]
    rev x3 -> x1, local copies, waits for them, and re-layouts: 18.8 us -> 0.06 us  [from_slots(): t = jnp.where(core == 1, jnp.flip(t, n + bits), t)]
    rev x2 -> x0, local copies, waits for them, and re-layouts: 16.4 us -> none  [to_slots(): t = jnp.where(core == 1, jnp.flip(t, n + bits), t)]
    select_n x10 -> x0, other arithmetic: 12.9 us -> none  [the longest x6 7.88 us: to_slots(): t = jnp.where(bit_of(chip, bit) == 1, jnp.flip(t, axis), t)]
  transfers between devices with their start and end apart: 84 -> 51, of which waited for: 27 -> 22; matrix products, arithmetic and copies ran while one was open for 27% -> 20% of each run, Pallas kernels for 7% -> 18%
where the time goes in v2:
time: 479 us; the launch traced here: 473 us
  waiting for transfers between devices  168 us (35%)
  Pallas kernels  142 us (30%)
  local copies, waits for them, and re-layouts  51.7 us (11%)
  starting transfers between devices  50.2 us (10%)
  other arithmetic  50.1 us (10%)
  between operations  9.68 us (2%)
    ppermute x14, waiting for transfers between devices, swap_narrow(): return lax.ppermute(v, 'narrow', [(z, z ^ mask) for z in range(size)])  106 us
    ppermute x37, waiting for transfers between devices, swap_wide(): return lax.ppermute(v, 'wide', [(w, w ^ mask) for w in range(size)])  62.6 us
    pallas_call x4, Pallas kernels, run_ffn_backward(): pl.pallas_call(functools.partial(ffn_backward, first, last, lax.axis_size...  45.4 us
    pallas_call x2, Pallas kernels, run_attend_backward(): pl.pallas_call(functools.partial(attend_backward, geometry, half), grid_s...  39 us
    ppermute x37, starting transfers between devices, swap_wide(): return lax.ppermute(v, 'wide', [(w, w ^ mask) for w in range(size)])  32.8 us
    pallas_call x2, Pallas kernels, run_ffn_forward(): pl.pallas_call(functools.partial(ffn_forward, first, last, lax.axis_size(...  32.1 us
    convert_element_type x25, other arithmetic, low_of(): return sum_of(parts, view).astype(bf16)  27.2 us
    pallas_call x1, Pallas kernels, run_attend_forward(): pl.pallas_call(functools.partial(attend_forward, geometry), grid_spec=plt...  22.1 us
  transfers between devices with their start and end apart: 51, of which 22 were waited for; matrix products, arithmetic and copies ran while one was open for 20% of the time, Pallas kernels for 18%

profile of v2, /device:TPU:0, one launch (start us, length us, event | category | flops | bytes accessed | tf_op | source)
XLA Modules:
  0.0 472.7 jit_solution(1179568464525576896)
XLA Ops:
  2.6 4.1 collective-permute-start.4
  6.7 12.6 %collective-permute-done.4 = bf16[1,136,1024]{2,1,0:T(8,128)(2,1)S(1)} collective-permute-done((bf16[1,136,1024]{2,1,0:T(8,128)(2,1)S(1)}, bf16[1,136,1024]{2,1,0:T(8,128)(2,1)S(1)}, u32[]{:S(2)}, u32[]{:S(2)}) %collective-permute-start.4) | collective-permute-done | bytes 278560 | tf_op jit(solution)/shard_map/ppermute | solution.py:41
  24.1 9.1 %collective-permute-done.5 = bf16[2,136,1024]{2,1,0:T(8,128)(2,1)S(1)} collective-permute-done((bf16[2,136,1024]{2,1,0:T(8,128)(2,1)S(1)}, bf16[2,136,1024]{2,1,0:T(8,128)(2,1)S(1)}, u32[]{:S(2)}, u32[]{:S(2)}) %collective-permute-start.5) | collective-permute-done | bytes 557088 | tf_op jit(solution)/shard_map/ppermute | solution.py:41
  44.8 8.9 %collective-permute-done.6 = bf16[2,128,768]{2,1,0:T(8,128)(2,1)S(1)} collective-permute-done((bf16[2,128,768]{2,1,0:T(8,128)(2,1)S(1)}, bf16[2,128,768]{2,1,0:T(8,128)(2,1)S(1)}, u32[]{:S(2)}, u32[]{:S(2)}) %collective-permute-start.6) | collective-permute-done | bytes 393248 | tf_op jit(solution)/shard_map/ppermute | solution.py:41
  57.0 13.1 %collective-permute-done.10 = bf16[4,136,512]{2,1,0:T(8,128)(2,1)S(1)} collective-permute-done((bf16[4,136,512]{2,1,0:T(8,128)(2,1)S(1)}, bf16[4,136,512]{2,1,0:T(8,128)(2,1)S(1)}, u32[]{:S(2)}, u32[]{:S(2)}) %collective-permute-start.10) | collective-permute-done | bytes 557088 | tf_op jit(solution)/shard_map/ppermute | solution.py:36
  84.9 9.4 %collective-permute-done.11 = bf16[2,4,136,512]{3,2,1,0:T(8,128)(2,1)S(1)} collective-permute-done((bf16[2,4,136,512]{3,2,1,0:T(8,128)(2,1)S(1)}, bf16[2,4,136,512]{3,2,1,0:T(8,128)(2,1)S(1)}, u32[]{:S(2)}, u32[]{:S(2)}) %collective-permute-start.11) | collective-permute-done | bytes 1114144 | tf_op jit(solution)/shard_map/ppermute | solution.py:36
  110.5 15.5 %collective-permute-done.9 = bf16[2,512,512]{2,1,0:T(8,128)(2,1)} collective-permute-done((bf16[2,512,512]{2,1,0:T(8,128)(2,1)}, bf16[2,512,512]{2,1,0:T(8,128)(2,1)}, u32[]{:S(2)}, u32[]{:S(2)}) %collective-permute-start.9) | collective-permute-done | bytes 1048608 | tf_op jit(solution)/shard_map/ppermute | solution.py:41
  139.6 22.1 %attend_forward.1 = (bf16[512,1024]{1,0:T(8,128)(2,1)}, bf16[512,1024]{1,0:T(8,128)(2,1)}, bf16[512,1024]{1,0:T(8,128)(2,1)}, bf16[16,512,512]{2,1,0:T(8,128)(2,...) custom-call(s32[3]{0:T(128)} %pad_add_fusion.pos.refs_0_, bf16[512,1024]{1,0:T(8,128)(2,1)} %x_ref, s32[1,512]{1,0:T(1,128)} %seg_row.1, ...), custom_call_target="tpu_custom_call" | custom-call | flops 8589934592 | bytes 25165824 | tf_op jit(solution)/shard_map/attend_forward/pallas_call | solution.py:246
  185.2 9.2 %ffn_forward.2 = (bf16[512,1024]{1,0:T(8,128)(2,1)}, bf16[512,1024]{1,0:T(8,128)(2,1)}, bf16[1024,512]{1,0:T(8,128)(2,1)}, f32[512,1024]{1,0:T(8,128)}) custom-call(s32[3]{0:T(128)} %pad_add_fusion.pos.refs_0_, f32[512,1024]{1,0:T(8,128)} %get-tuple-element.86.refs_1_.refs_12_, f32[8,1024]{1,0:T(8,128)} %permute.2.refs_2_.refs_13_, ...), custom_call_target="tpu_custom_call" | custom-call | flops 4294967296 | bytes 16777216 | tf_op jit(solution)/shard_map/ffn_forward/pallas_call | solution.py:563
  194.5 22.8 %ffn_forward.3 = (bf16[512,3072]{1,0:T(8,128)(2,1)}, bf16[512,3072]{1,0:T(8,128)(2,1)}, bf16[512,1024]{1,0:T(8,128)(2,1)}, f32[512,1024]{1,0:T(8,128)}, bf16[512...) custom-call(s32[3]{0:T(128)} %pad_add_fusion.pos.refs_0_, ...), custom_call_target="tpu_custom_call" | custom-call | flops 12884901888 | bytes 16777216 | tf_op jit(solution)/shard_map/ffn_forward/pallas_call | solution.py:563
  217.3 10.0 %ffn_backward.4 = (bf16[4,2,128,1024]{3,2,1,0:T(8,128)(2,1)}, bf16[4,2,128,1024]{3,2,1,0:T(8,128)(2,1)}, f32[1,1024]{1,0:T(1,128)}, f32[512,1024]{1,0:T(8,128)}) custom-call(s32[3]{0:T(128)} %pad_add_fusion.pos.refs_0_, bf16[512,1024]{1,0:T(8,128)(2,1)} %get-tuple-element.106.refs_1_, bf16[1024,512]{1,0:T(8,128)(2,1)} %get-tuple-element.94.refs_2_, ...), custom_call_target="tpu_custom_call" | custom-call | flops 4294967296 | bytes 16777216 | tf_op jit(solution)/shard_map/ffn_backward/pallas_call | solution.py:680
  227.9 10.6 %ffn_backward.5 = (bf16[4,2,128,1024]{3,2,1,0:T(8,128)(2,1)}, bf16[4,2,128,1024]{3,2,1,0:T(8,128)(2,1)}, f32[1,1024]{1,0:T(1,128)}, f32[512,1024]{1,0:T(8,128)}) custom-call(s32[3]{0:T(128)} %pad_add_fusion.pos.refs_0_, bf16[512,1024]{1,0:T(8,128)(2,1)} %get-tuple-element.106.refs_1_, bf16[1024,512]{1,0:T(8,128)(2,1)} %get-tuple-element.94.refs_2_, ...), custom_call_target="tpu_custom_call" | custom-call | flops 4294967296 | bytes 16777216 | tf_op jit(solution)/shard_map/ffn_backward/pallas_call | solution.py:680
  244.7 10.8 %ffn_backward.6 = (bf16[4,2,128,1024]{3,2,1,0:T(8,128)(2,1)}, bf16[4,2,128,1024]{3,2,1,0:T(8,128)(2,1)}, f32[1,1024]{1,0:T(1,128)}, f32[512,1024]{1,0:T(8,128)}) custom-call(s32[3]{0:T(128)} %pad_add_fusion.pos.refs_0_, bf16[512,1024]{1,0:T(8,128)(2,1)} %get-tuple-element.106.refs_1_, bf16[1024,512]{1,0:T(8,128)(2,1)} %get-tuple-element.94.refs_2_, ...), custom_call_target="tpu_custom_call" | custom-call | flops 4294967296 | bytes 16777216 | tf_op jit(solution)/shard_map/ffn_backward/pallas_call | solution.py:680
  255.5 13.9 %ffn_backward.7 = (bf16[4,2,128,1024]{3,2,1,0:T(8,128)(2,1)}, bf16[4,2,128,1024]{3,2,1,0:T(8,128)(2,1)}, f32[1,1024]{1,0:T(1,128)}, f32[512,1024]{1,0:T(8,128)}, f32[8,1024]{1,0:T(8,128)}) custom-call(s32[3]{0:T(128)} %pad_add_fusion.pos.refs_0_, bf16[512,1024]{1,0:T(8,128)(2,1)} %get-tuple-element.106.refs_1_, bf16[1024,512]{1,0:T(8,128)(2,1)} %get-tuple-element.94.refs_2_, ...), custom_call_target="tpu_custom_call" | custom-call | flops 4294967296 | bytes 16777216 | tf_op jit(solution)/shard_map/ffn_backward/pallas_call | solution.py:680
  283.8 23.3 %collective-permute-done.30 = bf16[2,2,2,128,512]{4,3,2,1,0:T(8,128)(2,1)} collective-permute-done((bf16[2,2,2,128,512]{4,3,2,1,0:T(8,128)(2,1)}, bf16[2,2,2,128,512]{4,3,2,1,0:T(8,128)(2,1)}, u32[]{:S(2)}, u32[]{:S(2)}) %collective-permute-start.30) | collective-permute-done | bytes 1048608 | tf_op jit(solution)/shard_map/ppermute | solution.py:41
  308.5 3.4 collective-permute-start.31
  321.5 13.1 %collective-permute-done.31 = bf16[2,2,2,128,256]{4,3,2,1,0:T(8,128)(2,1)S(1)} collective-permute-done((bf16[2,2,2,128,256]{4,3,2,1,0:T(8,128)(2,1)S(1)}, bf16[2,2,2,128,256]{4,3,2,1,0:T(8,128)(2,1)S(1)}, u32[]{:S(2)}, u32[]{:S(2)}) %collective-permute-start.31) | collective-permute-done | bytes 524320 | tf_op jit(solution)/shard_map/ppermute | solution.py:41
  336.5 19.9 %attend_backward.2 = (bf16[4,512,512]{2,1,0:T(8,128)(2,1)}, bf16[4,512,512]{2,1,0:T(8,128)(2,1)}, f32[512,1024]{1,0:T(8,128)}, f32[8,512]{1,0:T(8,128)}) custom-call(s32[3]{0:T(128)} %pad_add_fusion.pos.refs_0_, f32[512,1024]{1,0:T(8,128)} %get-tuple-element.116.dh_ref.add_ref, f32[512,1024]{1,0:T(8,128)} %get-tuple-element.116.dh_ref.add_ref, ...), custom_call_target="tpu_custom_call" | custom-call | flops 6442450944 | bytes 16777216 | tf_op jit(solution)/shard_map/attend_backward/pallas_call | solution.py:383
  363.7 19.1 %attend_backward.3 = (bf16[4,512,512]{2,1,0:T(8,128)(2,1)}, bf16[4,512,512]{2,1,0:T(8,128)(2,1)}, f32[512,1024]{1,0:T(8,128)}, f32[8,512]{1,0:T(8,128)}) custom-call(s32[3]{0:T(128)} %pad_add_fusion.pos.refs_0_, f32[512,1024]{1,0:T(8,128)} %get-tuple-element.116.dh_ref.add_ref, f32[512,1024]{1,0:T(8,128)} %get-tuple-element.121.add_ref, ...), custom_call_target="tpu_custom_call" | custom-call | flops 6442450944 | bytes 16777216 | tf_op jit(solution)/shard_map/attend_backward/pallas_call | solution.py:383
  405.2 19.8 %collective-permute-done.34 = bf16[2,2,2,128,512]{4,3,2,1,0:T(8,128)(2,1)S(1)} collective-permute-done((bf16[2,2,2,128,512]{4,3,2,1,0:T(8,128)(2,1)S(1)}, bf16[2,2,2,128,512]{4,3,2,1,0:T(8,128)(2,1)S(1)}, u32[]{:S(2)}, u32[]{:S(2)}) %collective-permute-start.34) | collective-permute-done | bytes 1048608 | tf_op jit(solution)/shard_map/ppermute | solution.py:36
  432.3 6.9 %collective-permute-done.35 = bf16[2,2,128,512]{3,2,1,0:T(8,128)(2,1)S(1)} collective-permute-done((bf16[2,2,128,512]{3,2,1,0:T(8,128)(2,1)S(1)}, bf16[2,2,128,512]{3,2,1,0:T(8,128)(2,1)S(1)}, u32[]{:S(2)}, u32[]{:S(2)}) %collective-permute-start.35) | collective-permute-done | bytes 524320 | tf_op jit(solution)/shard_map/ppermute | solution.py:36
  442.7 8.1 %collective-permute-done.48 = bf16[2,128,768]{2,1,0:T(8,128)(2,1)S(1)} collective-permute-done((bf16[2,128,768]{2,1,0:T(8,128)(2,1)S(1)}, bf16[2,128,768]{2,1,0:T(8,128)(2,1)S(1)}, u32[]{:S(2)}, u32[]{:S(2)}) %collective-permute-start.48) | collective-permute-done | bytes 393248 | tf_op jit(solution)/shard_map/ppermute | solution.py:41
  457.5 4.7 collective-permute-done.42
  464.8 5.6 %collective-permute-done.43 = bf16[136,512]{1,0:T(8,128)(2,1)S(1)} collective-permute-done((bf16[136,512]{1,0:T(8,128)(2,1)S(1)}, bf16[136,512]{1,0:T(8,128)(2,1)S(1)}, u32[]{:S(2)}, u32[]{:S(2)}) %collective-permute-start.43) | collective-permute-done | bytes 139296 | tf_op jit(solution)/shard_map/ppermute | solution.py:41
  (342 shorter events, 167.0 us)
Async XLA Ops:
  56.5 38.1 %collective-permute-start.14 = (bf16[2,4,128,512]{3,2,1,0:T(8,128)(2,1)S(1)}, bf16[2,4,128,512]{3,2,1,0:T(8,128)(2,1)S(1)}, u32[]{:S(2)}, u32[]{:S(2)}) collective-permute-start(bf16[2,4,128,512]{3,2,1,0:T(8,128)(2,1)S(1)} %get-tuple-element.184), channel_id=1, source_target_pairs={{0,8},{4,12},{8,0},{12,4},{16,24},{20,28},{24,16},{28,20},{1,9},{5... | collective-permute-start | bytes 3145736 | tf_op jit(solution)/shard_map/ppermute | solution.py:36
  70.3 24.0 %collective-permute-start.11 = (bf16[2,4,136,512]{3,2,1,0:T(8,128)(2,1)S(1)}, bf16[2,4,136,512]{3,2,1,0:T(8,128)(2,1)S(1)}, u32[]{:S(2)}, u32[]{:S(2)}) collective-permute-start(bf16[2,4,136,512]{3,2,1,0:T(8,128)(2,1)S(1)} %get-tuple-element.178), channel_id=1, source_target_pairs={{0,16},{4,20},{8,24},{12,28},{16,0},{20,4},{24,8},{28,12},{1,17},{... | collective-permute-start | bytes 3342344 | tf_op jit(solution)/shard_map/ppermute | solution.py:36
  73.1 26.6 %collective-permute-start.8 = (bf16[2,512,256]{2,1,0:T(8,128)(2,1)S(1)}, bf16[2,512,256]{2,1,0:T(8,128)(2,1)S(1)}, u32[]{:S(2)}, u32[]{:S(2)}) collective-permute-start(bf16[2,512,256]{2,1,0:T(8,128)(2,1)S(1)} %pad_maximum_fusion.16), channel_id=1, source_target_pairs={{0,2},{1,3},{2,0},{3,1},{4,6},{5,7},{6,4},{7,5},{8,10},{9,11},{10,... | collective-permute-start | bytes 1572872 | tf_op jit(solution)/shard_map/ppermute | solution.py:41
  100.8 25.2 %collective-permute-start.9 = (bf16[2,512,512]{2,1,0:T(8,128)(2,1)}, bf16[2,512,512]{2,1,0:T(8,128)(2,1)}, u32[]{:S(2)}, u32[]{:S(2)}) collective-permute-start(bf16[2,512,512]{2,1,0:T(8,128)(2,1)} %pad_maximum_fusion.9), channel_id=1, source_target_pairs={{0,1},{1,0},{2,3},{3,2},{4,5},{5,4},{6,7},{7,6},{8,9},{9,8},{10,11... | collective-permute-start | bytes 3145736 | tf_op jit(solution)/shard_map/ppermute | solution.py:41
  104.2 25.1 %collective-permute-start.16 = (bf16[128,3072]{1,0:T(8,128)(2,1)}, bf16[128,3072]{1,0:T(8,128)(2,1)}, u32[]{:S(2)}, u32[]{:S(2)}) collective-permute-start(bf16[128,3072]{1,0:T(8,128)(2,1)} %get-tuple-element.87), channel_id=1, source_target_pairs={{0,8},{4,12},{8,0},{12,4},{16,24},{20,28},{24,16},{28,20},{1,9},{5... | collective-permute-start | bytes 2359304 | tf_op jit(solution)/shard_map/ppermute | solution.py:36
  109.0 24.7 %collective-permute-start.19 = (bf16[128,3072]{1,0:T(8,128)(2,1)}, bf16[128,3072]{1,0:T(8,128)(2,1)S(1)}, u32[]{:S(2)}, u32[]{:S(2)}) collective-permute-start(bf16[128,3072]{1,0:T(8,128)(2,1)} %get-tuple-element.89), channel_id=1, source_target_pairs={{0,16},{4,20},{8,24},{12,28},{16,0},{20,4},{24,8},{28,12},{1,17},{... | collective-permute-start | bytes 2359304 | tf_op jit(solution)/shard_map/ppermute | solution.py:36
  132.0 35.3 %collective-permute-start.17 = (bf16[2,128,3072]{2,1,0:T(8,128)(2,1)S(1)}, bf16[2,128,3072]{2,1,0:T(8,128)(2,1)}, u32[]{:S(2)}, u32[]{:S(2)}) collective-permute-start(bf16[2,128,3072]{2,1,0:T(8,128)(2,1)S(1)} %get-tuple-element.167), channel_id=1, source_target_pairs={{0,16},{4,20},{8,24},{12,28},{16,0},{20,4},{24,8},{28,12},{1,17},{... | collective-permute-start | bytes 4718600 | tf_op jit(solution)/shard_map/ppermute | solution.py:36
  136.8 35.3 %collective-permute-start.20 = (bf16[2,128,3072]{2,1,0:T(8,128)(2,1)}, bf16[2,128,3072]{2,1,0:T(8,128)(2,1)}, u32[]{:S(2)}, u32[]{:S(2)}) collective-permute-start(bf16[2,128,3072]{2,1,0:T(8,128)(2,1)} %get-tuple-element.159), channel_id=1, source_target_pairs={{0,8},{4,12},{8,0},{12,4},{16,24},{20,28},{24,16},{28,20},{1,9},{5... | collective-permute-start | bytes 4718600 | tf_op jit(solution)/shard_map/ppermute | solution.py:36
  169.2 25.3 %collective-permute-start.18 = (bf16[512,3072]{1,0:T(8,128)(2,1)S(1)}, bf16[512,3072]{1,0:T(8,128)(2,1)}, u32[]{:S(2)}, u32[]{:S(2)}) collective-permute-start(bf16[512,3072]{1,0:T(8,128)(2,1)S(1)} %bitcast.437), channel_id=1, source_target_pairs={{0,4},{4,0},{8,12},{12,8},{16,20},{20,16},{24,28},{28,24},{1,5},{5... | collective-permute-start | bytes 9437192 | tf_op jit(solution)/shard_map/ppermute | solution.py:36
  269.4 46.7 %collective-permute-start.28 = (bf16[4,2,128,1024]{3,2,1,0:T(8,128)(2,1)}, bf16[4,2,128,1024]{3,2,1,0:T(8,128)(2,1)}, u32[]{:S(2)}, u32[]{:S(2)}) collective-permute-start(bf16[4,2,128,1024]{3,2,1,0:T(8,128)(2,1)} %get-tuple-element.114), channel_id=1, source_target_pairs={{0,4},{4,0},{8,12},{12,8},{16,20},{20,16},{24,28},{28,24},{1,5},{5... | collective-permute-start | bytes 6291464 | tf_op jit(solution)/shard_map/ppermute | solution.py:36
  277.9 40.4 %collective-permute-start.26 = (bf16[4,2,128,1024]{3,2,1,0:T(8,128)(2,1)}, bf16[4,2,128,1024]{3,2,1,0:T(8,128)(2,1)}, u32[]{:S(2)}, u32[]{:S(2)}) collective-permute-start(bf16[4,2,128,1024]{3,2,1,0:T(8,128)(2,1)} %get-tuple-element.112), channel_id=1, source_target_pairs={{0,4},{4,0},{8,12},{12,8},{16,20},{20,16},{24,28},{28,24},{1,5},{5... | collective-permute-start | bytes 6291464 | tf_op jit(solution)/shard_map/ppermute | solution.py:36
  281.6 25.5 %collective-permute-start.30 = (bf16[2,2,2,128,512]{4,3,2,1,0:T(8,128)(2,1)}, bf16[2,2,2,128,512]{4,3,2,1,0:T(8,128)(2,1)}, u32[]{:S(2)}, u32[]{:S(2)}) collective-permute-start(bf16[2,2,2,128,512]{4,3,2,1,0:T(8,128)(2,1)} %add_convert_fusion.5), channel_id=1, source_target_pairs={{0,1},{1,0},{2,3},{3,2},{4,5},{5,4},{6,7},{7,6},{8,9},{9,8},{10,11... | collective-permute-start | bytes 3145736 | tf_op jit(solution)/shard_map/ppermute | solution.py:41
  282.1 29.8 %collective-permute-start.32 = (bf16[2,2,128,1024]{3,2,1,0:T(8,128)(2,1)}, bf16[2,2,128,1024]{3,2,1,0:T(8,128)(2,1)S(1)}, u32[]{:S(2)}, u32[]{:S(2)}) collective-permute-start(bf16[2,2,128,1024]{3,2,1,0:T(8,128)(2,1)} %add_convert_fusion.4), channel_id=1, source_target_pairs={{0,16},{4,20},{8,24},{12,28},{16,0},{20,4},{24,8},{28,12},{1,17},{... | collective-permute-start | bytes 3145736 | tf_op jit(solution)/shard_map/ppermute | solution.py:36
  308.5 26.1 %collective-permute-start.31 = (bf16[2,2,2,128,256]{4,3,2,1,0:T(8,128)(2,1)S(1)}, bf16[2,2,2,128,256]{4,3,2,1,0:T(8,128)(2,1)S(1)}, u32[]{:S(2)}, u32[]{:S(2)}) collective-permute-start(bf16[2,2,2,128,256]{4,3,2,1,0:T(8,128)(2,1)S(1)} %add_convert_fusion.7), channel_id=1, source_target_pairs={{0,2},{1,3},{2,0},{3,1},{4,6},{5,7},{6,4},{7,5},{8,10},{9,11},{10,... | collective-permute-start | bytes 1572872 | tf_op jit(solution)/shard_map/ppermute | solution.py:41
  314.6 76.6 %collective-permute-start.44 = (bf16[2,128,1024]{2,1,0:T(8,128)(2,1)}, bf16[2,128,1024]{2,1,0:T(8,128)(2,1)}, u32[]{:S(2)}, u32[]{:S(2)}) collective-permute-start(bf16[2,128,1024]{2,1,0:T(8,128)(2,1)} %fusion.7), channel_id=1, source_target_pairs={{0,8},{4,12},{8,0},{12,4},{16,24},{20,28},{24,16},{28,20},{1,9},{5... | collective-permute-start | bytes 1572872 | tf_op jit(solution)/shard_map/ppermute | solution.py:36
  317.8 39.7 %collective-permute-start.29 = (bf16[2,2,128,1024]{3,2,1,0:T(8,128)(2,1)S(1)}, bf16[2,2,128,1024]{3,2,1,0:T(8,128)(2,1)}, u32[]{:S(2)}, u32[]{:S(2)}) collective-permute-start(bf16[2,2,128,1024]{3,2,1,0:T(8,128)(2,1)S(1)} %add_convert_fusion.2), channel_id=1, source_target_pairs={{0,16},{4,20},{8,24},{12,28},{16,0},{20,4},{24,8},{28,12},{1,17},{... | collective-permute-start | bytes 3145736 | tf_op jit(solution)/shard_map/ppermute | solution.py:36
  320.9 40.4 %collective-permute-start.27 = (bf16[2,2,128,1024]{3,2,1,0:T(8,128)(2,1)}, bf16[2,2,128,1024]{3,2,1,0:T(8,128)(2,1)}, u32[]{:S(2)}, u32[]{:S(2)}) collective-permute-start(bf16[2,2,128,1024]{3,2,1,0:T(8,128)(2,1)} %fusion), channel_id=1, source_target_pairs={{0,8},{4,12},{8,0},{12,4},{16,24},{20,28},{24,16},{28,20},{1,9},{5... | collective-permute-start | bytes 3145736 | tf_op jit(solution)/shard_map/ppermute | solution.py:36
  336.0 55.2 %collective-permute-start.49 = (bf16[2,2,128,256]{3,2,1,0:T(8,128)(2,1)S(1)}, bf16[2,2,128,256]{3,2,1,0:T(8,128)(2,1)}, u32[]{:S(2)}, u32[]{:S(2)}) collective-permute-start(bf16[2,2,128,256]{3,2,1,0:T(8,128)(2,1)S(1)} %fusion.10), channel_id=1, source_target_pairs={{0,16},{4,20},{8,24},{12,28},{16,0},{20,4},{24,8},{28,12},{1,17},{... | collective-permute-start | bytes 786440 | tf_op jit(solution)/shard_map/ppermute | solution.py:36
  357.1 41.4 %collective-permute-start.33 = (bf16[4,512,512]{2,1,0:T(8,128)(2,1)}, bf16[4,512,512]{2,1,0:T(8,128)(2,1)}, u32[]{:S(2)}, u32[]{:S(2)}) collective-permute-start(bf16[4,512,512]{2,1,0:T(8,128)(2,1)} %get-tuple-element.124), channel_id=1, source_target_pairs={{0,4},{4,0},{8,12},{12,8},{16,20},{20,16},{24,28},{28,24},{1,5},{5... | collective-permute-start | bytes 6291464 | tf_op jit(solution)/shard_map/ppermute | solution.py:36
  359.9 43.9 %collective-permute-start.46 = (bf16[2,128,1024]{2,1,0:T(8,128)(2,1)}, bf16[2,128,1024]{2,1,0:T(8,128)(2,1)S(1)}, u32[]{:S(2)}, u32[]{:S(2)}) collective-permute-start(bf16[2,128,1024]{2,1,0:T(8,128)(2,1)} %fusion.6), channel_id=1, source_target_pairs={{0,8},{4,12},{8,0},{12,4},{16,24},{20,28},{24,16},{28,20},{1,9},{5... | collective-permute-start | bytes 1572872 | tf_op jit(solution)/shard_map/ppermute | solution.py:36
  397.9 31.6 %collective-permute-start.50 = (bf16[2,128,256]{2,1,0:T(8,128)(2,1)S(1)}, bf16[2,128,256]{2,1,0:T(8,128)(2,1)S(1)}, u32[]{:S(2)}, u32[]{:S(2)}) collective-permute-start(bf16[2,128,256]{2,1,0:T(8,128)(2,1)S(1)} %fusion.11), channel_id=1, source_target_pairs={{0,8},{4,12},{8,0},{12,4},{16,24},{20,28},{24,16},{28,20},{1,9},{5... | collective-permute-start | bytes 393224 | tf_op jit(solution)/shard_map/ppermute | solution.py:36
  400.1 25.0 %collective-permute-start.34 = (bf16[2,2,2,128,512]{4,3,2,1,0:T(8,128)(2,1)S(1)}, bf16[2,2,2,128,512]{4,3,2,1,0:T(8,128)(2,1)S(1)}, u32[]{:S(2)}, u32[]{:S(2)}) collective-permute-start(bf16[2,2,2,128,512]{4,3,2,1,0:T(8,128)(2,1)S(1)} %fusion.1), channel_id=1, source_target_pairs={{0,16},{4,20},{8,24},{12,28},{16,0},{20,4},{24,8},{28,12},{1,17},{... | collective-permute-start | bytes 3145736 | tf_op jit(solution)/shard_map/ppermute | solution.py:36
  401.1 26.7 %collective-permute-start.40 = (bf16[2,2,2,136,512]{4,3,2,1,0:T(8,128)(2,1)S(1)}, bf16[2,2,2,136,512]{4,3,2,1,0:T(8,128)(2,1)S(1)}, u32[]{:S(2)}, u32[]{:S(2)}) collective-permute-start(bf16[2,2,2,136,512]{4,3,2,1,0:T(8,128)(2,1)S(1)} %pad_maximum_fusion.8), channel_id=1, source_target_pairs={{0,8},{4,12},{8,0},{12,4},{16,24},{20,28},{24,16},{28,20},{1,9},{5... | collective-permute-start | bytes 3342344 | tf_op jit(solution)/shard_map/ppermute | solution.py:36
  405.1 25.6 %collective-permute-start.47 = (bf16[2,128,1536]{2,1,0:T(8,128)(2,1)S(1)}, bf16[2,128,1536]{2,1,0:T(8,128)(2,1)S(1)}, u32[]{:S(2)}, u32[]{:S(2)}) collective-permute-start(bf16[2,128,1536]{2,1,0:T(8,128)(2,1)S(1)} %pad_maximum_fusion.13), channel_id=1, source_target_pairs={{0,1},{1,0},{2,3},{3,2},{4,5},{5,4},{6,7},{7,6},{8,9},{9,8},{10,11... | collective-permute-start | bytes 2359304 | tf_op jit(solution)/shard_map/ppermute | solution.py:41
  (51 other events, 539.0 us)
